TPU v7x, 256 devices: a whole 4x4x8 slice. The times are simulated.
256 devices in a mesh: enc: 16 (over z, core), dec: 4 (over x), mp: 4 (over y).
Axes of the slice: x: 4, y: 4, z: 8, core: 2. Of those that a mesh axis runs over, the one named last changes fastest.
Arguments:
- encoded: bfloat16 [1024, 32, 4096], P(('enc', 'dec')), may hold values from -6 to 6
- owner: int32 [1024], P(('enc', 'dec')), may hold values from -1 to 63, as said below
- key_weight: bfloat16 [4096, 2048], P(('enc', 'dec'), 'mp'), may hold values from -0.09375 to 0.09375
- value_weight: bfloat16 [4096, 2048], P(('enc', 'dec'), 'mp'), may hold values from -0.09375 to 0.09375
- queries: bfloat16 [64, 64, 2048], P(('enc', 'dec'), None, 'mp'), may hold values from -7 to 7
- grad_context: bfloat16 [64, 64, 2048], P(('enc', 'dec'), None, 'mp'), may hold values from -6 to 6
Outputs:
- context: bfloat16 [64, 64, 2048], P(('enc', 'dec'), None, 'mp')
- grad_queries: bfloat16 [64, 64, 2048], P(('enc', 'dec'), None, 'mp')
- grad_encoded: bfloat16 [1024, 32, 4096], P(('enc', 'dec'))
Inputs may be any that keep to these rules, and one draw needn't show every extreme that they name: `owner`: slot p lies on device group p // 16 of enc+dec (group index enc * 4 + dec), and question q is owned by group q. A live slot's question has the same dec index as the slot's group. Each question has 4 to 16 passages; one device group holds at most 2 passages of one question, and every question has exactly 2 on some group. In every dec row some group has all 16 slots live.
All inputs are finite; a program needn't handle non-finite values.
Results may differ from a plain program's by a relative error of at most 0.04.
The roundings to bfloat16 on the way count: a program that leaves them out, or rounds other values in their place, can miss the bound.
Values may be sent and summed in bfloat16 or wider, within the bound.
A program may use at most 64 MiB of HBM per device.

v0:
```python
import jax
import jax.numpy as jnp
from jax import lax
from jax.sharding import PartitionSpec as P

HEAD_DIM = 64
MOST = 16


def attend(query_rows, key_rows, value_rows, grad_rows, key_live):
    scores = jnp.einsum("thd,shd->hts", query_rows, key_rows, preferred_element_type=jnp.float32)
    scores = jnp.where(key_live[None, None, :], scores, -jnp.inf)
    row_peak = jnp.max(scores, axis=-1, keepdims=True)
    raised = jnp.exp(scores - row_peak)
    chances = raised / jnp.sum(raised, axis=-1, keepdims=True)
    chances_low = chances.astype(jnp.bfloat16)
    context = jnp.einsum(
        "hts,shd->thd", chances_low, value_rows, preferred_element_type=jnp.float32
    )
    grad_chances = jnp.einsum(
        "thd,shd->hts", grad_rows, value_rows, preferred_element_type=jnp.float32
    )
    row_delta = jnp.sum(chances * grad_chances, axis=-1, keepdims=True)
    grad_scores = (chances * (grad_chances - row_delta)).astype(jnp.bfloat16)
    grad_query = jnp.einsum(
        "hts,shd->thd", grad_scores, key_rows, preferred_element_type=jnp.float32
    )
    grad_key = jnp.einsum(
        "hts,thd->shd", grad_scores, query_rows, preferred_element_type=jnp.float32
    )
    grad_value = jnp.einsum(
        "hts,thd->shd", chances_low, grad_rows, preferred_element_type=jnp.float32
    )
    return (
        context.astype(jnp.bfloat16),
        grad_query.astype(jnp.bfloat16),
        grad_key.astype(jnp.bfloat16),
        grad_value.astype(jnp.bfloat16),
    )


def on_device(encoded, owner, key_weight, value_weight, queries, grad_context):
    enc_count = lax.axis_size("enc")
    dec_count = lax.axis_size("dec")
    slot_count, length, model_width = encoded.shape
    head_width = key_weight.shape[1]
    heads_here = head_width // HEAD_DIM
    target_len = queries.shape[1]
    capacity = MOST // min(8, enc_count)
    flat_rows = encoded.reshape(slot_count * length, model_width)
    local_pair = jnp.concatenate([key_weight, value_weight], axis=1)
    projected = jnp.dot(
        flat_rows,
        lax.all_gather(local_pair, ("enc", "dec"), axis=0, tiled=True),
        preferred_element_type=jnp.float32,
    )
    key_value = projected.astype(jnp.bfloat16).reshape(slot_count, length * 2 * head_width)
    is_live = owner >= 0
    target = jnp.where(is_live, owner // dec_count, 0)
    earlier = jnp.arange(slot_count)[:, None] > jnp.arange(slot_count)[None, :]
    same_owner = (target[:, None] == target[None, :]) & is_live[None, :] & earlier
    position = jnp.sum(same_owner.astype(jnp.int32), axis=1)
    slot_target = jnp.where(is_live, target * capacity + position, -1)
    selector = (jnp.arange(enc_count * capacity)[:, None] == slot_target[None, :]).astype(
        jnp.bfloat16
    )
    outgoing = jnp.dot(selector, key_value, preferred_element_type=jnp.float32).astype(jnp.bfloat16)
    outgoing = outgoing.reshape(enc_count, capacity, length, 2 * head_width)
    live_slots = (
        jnp.sum(selector.astype(jnp.float32), axis=1)
        .astype(jnp.bfloat16)
        .reshape(enc_count, capacity)
    )
    received, received_live = (
        lax.all_to_all(outgoing, "enc", split_axis=0, concat_axis=0, tiled=True),
        lax.all_to_all(live_slots, "enc", split_axis=0, concat_axis=0, tiled=True),
    )
    key_count = enc_count * capacity * length
    received_rows = received.reshape(key_count, 2 * head_width)
    key_rows = received_rows[:, :head_width].reshape(key_count, heads_here, HEAD_DIM)
    value_rows = received_rows[:, head_width:].reshape(key_count, heads_here, HEAD_DIM)
    key_live = (
        jnp.broadcast_to(received_live[:, :, None], (enc_count, capacity, length)).reshape(
            key_count
        )
        > 0.5
    )
    query_rows = queries.reshape(target_len, heads_here, HEAD_DIM)
    grad_rows = grad_context.reshape(target_len, heads_here, HEAD_DIM)
    context, grad_query, grad_key, grad_value = attend(
        query_rows, key_rows, value_rows, grad_rows, key_live
    )
    returning = jnp.concatenate(
        [grad_key.reshape(key_count, head_width), grad_value.reshape(key_count, head_width)], axis=1
    )
    returning = returning.reshape(enc_count, capacity, length, 2 * head_width)
    arrived = lax.all_to_all(returning, "enc", split_axis=0, concat_axis=0, tiled=True)
    arrived = arrived.reshape(enc_count * capacity, length * 2 * head_width)
    grad_pair = lax.dot_general(
        selector, arrived, (((0,), (0,)), ((), ())), preferred_element_type=jnp.float32
    )
    grad_pair = grad_pair.astype(jnp.bfloat16).reshape(slot_count * length, 2 * head_width)
    partial_sum = lax.dot_general(
        grad_pair,
        lax.all_gather(local_pair, ("enc", "dec"), axis=0, tiled=True),
        (((1,), (1,)), ((), ())),
        preferred_element_type=jnp.float32,
    )
    grad_flat = lax.psum(partial_sum.astype(jnp.bfloat16), "mp")
    grad_encoded = grad_flat.reshape(slot_count, length, model_width)
    return (context.reshape(queries.shape), grad_query.reshape(queries.shape), grad_encoded)


def solution(mesh):
    in_specs = (
        P(("enc", "dec"), None, None),
        P(("enc", "dec")),
        P(("enc", "dec"), "mp"),
        P(("enc", "dec"), "mp"),
        P(("enc", "dec"), None, "mp"),
        P(("enc", "dec"), None, "mp"),
    )
    out_specs = (
        P(("enc", "dec"), None, "mp"),
        P(("enc", "dec"), None, "mp"),
        P(("enc", "dec"), None, None),
    )
    return jax.shard_map(
        on_device, mesh=mesh, in_specs=in_specs, out_specs=out_specs, check_vma=False
    )
```

profile of v0, /device:TPU:1, one launch (start us, length us, event | category | flops | bytes accessed | tf_op | source)
XLA Modules:
  0.0 364.1 jit_solution(5578889976012949103)
XLA Ops:
  7.2 1.5 pad_maximum_fusion.1
  11.7 10.0 %all-to-all-start.1 = ((bf16[16,1,2]{2,1,0:T(2,128)(2,1)}), bf16[16,1,2]{2,1,0:T(2,128)(2,1)S(1)}, u32[]{:S(2)}, u32[]{:S(2)}) async-start(bf16[16,1,2]{2,1,0:T(2,128)(2,1)} %all_to_all.16), calls=%async_computation.1 | async-start | bytes 16384 | tf_op jit(solution)/shard_map/all_to_all | solution.py:76
  21.7 76.8 %all-gather.2.cloned.1.call-done = bf16[4096,1024]{1,0:T(8,128)(2,1)} async-done(((bf16[64,1024]{1,0:T(8,128)(2,1)}), bf16[4096,1024]{1,0:T(8,128)(2,1)}) %all-gather.2.cloned.1.call-update) | async-done | bytes 8388624 | tf_op jit(solution)/shard_map/all_gather | solution.py:54
  98.5 9.1 %fusion.11 = bf16[512,1024]{0,1:T(8,128)(2,1)S(1)} fusion(bf16[4096,1024]{1,0:T(8,128)(2,1)} %all-gather.2.cloned.1.call-done, bf16[512,4096]{1,0:T(8,128)(2,1)} %bitcast.81), kind=kOutput, calls=%fused_computation.20 | convolution fusion | flops 4295491584 | bytes 13631488 | tf_op jit(solution)/shard_map/dot_general | solution.py:52
  109.5 2.5 copy.78
  112.0 5.0 %all-to-all-start = ((bf16[16,2,32,1024]{3,2,1,0:T(8,128)(2,1)}), bf16[16,2,32,1024]{3,2,1,0:T(8,128)(2,1)S(1)}, u32[]{:S(2)}, u32[]{:S(2)}) async-start(bf16[16,2,32,1024]{3,2,1,0:T(8,128)(2,1)} %bitcast.68), calls=%async_computation | async-start | bytes 4194304 | tf_op jit(solution)/shard_map/all_to_all | solution.py:75
  117.8 48.1 %all-to-all-done = bf16[16,2,32,1024]{3,2,1,0:T(8,128)(2,1)S(1)} async-done(((bf16[16,2,32,1024]{3,2,1,0:T(8,128)(2,1)}), bf16[16,2,32,1024]{3,2,1,0:T(8,128)(2,1)S(1)}, u32[]{:S(2)}, u32[]{:S(2)}) %all-to-all-start) | async-done | bytes 2097184 | tf_op jit(solution)/shard_map/all_to_all | solution.py:75
  167.0 2.3 copy.74
  170.7 1.5 fusion.10
  172.6 1.9 fusion.1
  174.5 2.6 copy.71
  177.1 2.1 concatenate.13
  179.2 2.6 fusion.3
  182.2 2.5 copy.69
  184.7 4.1 %concatenate.12 = bf16[16,2,32,512]{3,2,1,0:T(8,128)(2,1)} reshape(bf16[1024,8,64]{2,1,0:T(8,128)(2,1)} %copy.69) | data formatting | bytes 2097152 | tf_op jit(solution)/shard_map/concatenate | solution.py:93
  188.8 1.5 pad_maximum_fusion
  190.3 55.8 %all_to_all.20 = bf16[16,2,32,1024]{3,2,1,0:T(8,128)(2,1)S(1)} all-to-all(bf16[16,2,32,1024]{3,2,1,0:T(8,128)(2,1)S(1)} %pad_maximum_fusion), channel_id=1, replica_groups=mesh['enc'=16,'dec'=4,'mp'=4] {'enc'}, dimensions={0} | all-to-all | bytes 4194304 | tf_op jit(solution)/shard_map/all_to_all | solution.py:97
  246.1 1.2 copy.79
  247.8 1.3 reshape.86
  249.1 10.3 %convolution_convert_fusion.2 = bf16[512,4096]{1,0:T(8,128)(2,1)} fusion(bf16[512,1024]{1,0:T(8,128)(2,1)} %reshape.86, bf16[4096,1024]{1,0:T(8,128)(2,1)} %all-gather.2.cloned.1.call-done), kind=kOutput, calls=%fused_computation.3 | convolution fusion | flops 4297064448 | bytes 13631488 | tf_op jit(solution)/shard_map/dot_general | solution.py:103
  259.4 1.2 copy-done.3
  260.6 2.1 convolution_convert_fusion.7
  264.6 88.0 %all-reduce.2.cloned.1.call-done = bf16[16,32,4096]{2,1,0:T(8,128)(2,1)} async-done(((bf16[16,32,4096]{2,1,0:T(8,128)(2,1)}), bf16[16,32,4096]{2,1,0:T(8,128)(2,1)}) %all-reduce.2.cloned.1.call-update) | async-done | bytes 4194320 | tf_op jit(solution)/shard_map/psum | solution.py:109
  352.6 4.7 %copy.81 = bf16[16,32,4096]{2,1,0:T(8,128)(2,1)} copy(bf16[16,32,4096]{2,1,0:T(8,128)(2,1)} %all-reduce.2.cloned.1.call-done) | data formatting | bytes 8388608
  (40 shorter events, 11.5 us)
Async XLA Ops:
  7.2 91.3 %all-gather.2.cloned.1.call-start = ((), (), s32[]{:S(2)}) async-start(), calls=%async_computation.3 | async-start | bytes 8519680 | tf_op jit(solution)/shard_map/all_gather | solution.py:54
  11.7 100.2 %all-to-all-start.1 = ((bf16[16,1,2]{2,1,0:T(2,128)(2,1)}), bf16[16,1,2]{2,1,0:T(2,128)(2,1)S(1)}, u32[]{:S(2)}, u32[]{:S(2)}) async-start(bf16[16,1,2]{2,1,0:T(2,128)(2,1)} %all_to_all.16), calls=%async_computation.1 | async-start | bytes 16384 | tf_op jit(solution)/shard_map/all_to_all | solution.py:76
  112.0 5.2 %copy-start.4 = (bf16[1,64,512]{2,1,0:T(8,128)(2,1)S(1)}, bf16[1,64,512]{2,1,0:T(8,128)(2,1)}, u32[]{:S(2)}) copy-start(bf16[1,64,512]{2,1,0:T(8,128)(2,1)} %param.10) | copy-start | bytes 196612
  112.0 5.3 %copy-start.5 = (bf16[1,64,512]{2,1,0:T(8,128)(2,1)S(1)}, bf16[1,64,512]{2,1,0:T(8,128)(2,1)}, u32[]{:S(2)}) copy-start(bf16[1,64,512]{2,1,0:T(8,128)(2,1)} %param.11) | copy-start | bytes 196612
  112.0 53.9 %all-to-all-start = ((bf16[16,2,32,1024]{3,2,1,0:T(8,128)(2,1)}), bf16[16,2,32,1024]{3,2,1,0:T(8,128)(2,1)S(1)}, u32[]{:S(2)}, u32[]{:S(2)}) async-start(bf16[16,2,32,1024]{3,2,1,0:T(8,128)(2,1)} %bitcast.68), calls=%async_computation | async-start | bytes 4194304 | tf_op jit(solution)/shard_map/all_to_all | solution.py:75
  117.0 235.6 %all-reduce.2.cloned.1.call-start = ((), (), s32[]{:S(2)}) async-start(), calls=%async_computation.4 | async-start | bytes 8388608 | tf_op jit(solution)/shard_map/psum | solution.py:109
  170.6 1.7 copy-start
  170.6 2.0 copy-start.2
  184.7 4.1 %copy-start.1 = (bf16[16,2,32,512]{3,2,1,0:T(8,128)(2,1)S(1)}, bf16[16,2,32,512]{3,2,1,0:T(8,128)(2,1)}, u32[]{:S(2)}) copy-start(bf16[16,2,32,512]{3,2,1,0:T(8,128)(2,1)} %concatenate.13) | copy-start | bytes 3145732
  259.4 1.2 copy-start.3
Sparse Core Ops, SparseCore 0:
  11.3 87.1 all-gather.1
  259.5 93.0 all-reduce.1
where the time goes:
time: 365 us; the launch traced here: 364 us
  waiting for transfers between devices  213 us (58%)
  blocking collectives  55.8 us (15%)
  local copies, waits for them, and re-layouts  30.5 us (8%)
  matrix products  27.7 us (8%)
  starting transfers between devices  15.2 us (4%)
  between operations  14.2 us (4%)
  other arithmetic  7.85 us (2%)
    psum x1, waiting for transfers between devices, on_device(): grad_flat = lax.psum(partial_sum.astype(jnp.bfloat16), 'mp')  88 us
    all_gather x1, waiting for transfers between devices, on_device(): lax.all_gather(local_pair, ('enc', 'dec'), axis=0, tiled=True)  76.8 us
    all_to_all x1, blocking collectives, on_device(): lax.all_to_all(returning, 'enc', split_axis=0, concat_axis=0, tiled=True)  55.8 us
    all_to_all x1, waiting for transfers between devices, on_device(): lax.all_to_all(outgoing, 'enc', split_axis=0, concat_axis=0, tiled=True)  48.1 us
    unnamed x19, local copies, waits for them, and re-layouts  14.3 us
    dot_general x1, matrix products, on_device(): lax.dot_general(grad_pair, lax.all_gather(local_pair, ('enc', 'dec'), axi...  10.3 us
    all_to_all x1, starting transfers between devices, on_device(): lax.all_to_all(live_slots, 'enc', split_axis=0, concat_axis=0, tiled=True)  9.98 us
    dot_general x1, matrix products, on_device(): jnp.dot(flat_rows, lax.all_gather(local_pair, ('enc', 'dec'), axis=0, til...  9.11 us
  transfers between devices with their start and end apart: 4, of which 3 were waited for; matrix products, arithmetic and copies ran while one was open for 6% of the time, Pallas kernels for 0%

commit v1 on v0

v1 whole, which is shorter than its diff:
```python
import functools

import jax
import jax.numpy as jnp
from jax import lax
from jax.experimental import pallas as pl
from jax.experimental.pallas import tpu as pltpu
from jax.sharding import PartitionSpec as P

HEAD_DIM = 64
GROUP = 4
WIDE = GROUP * HEAD_DIM
LOW = -1e30
MIB = 1024 * 1024
BF16 = jnp.bfloat16
F32 = jnp.float32

NT = (((1,), (1,)), ((), ()))
TN = (((0,), (0,)), ((), ()))


def remote(src, dst, send_sem, recv_sem, **where):
    return pltpu.make_async_remote_copy(
        src_ref=src,
        dst_ref=dst,
        send_sem=send_sem,
        recv_sem=recv_sem,
        device_id=where,
        device_id_type=pl.DeviceIdType.MESH,
    )


def greet(partners):
    barrier = pltpu.get_barrier_semaphore()
    for where in partners:
        pl.semaphore_signal(barrier, inc=1, device_id=where, device_id_type=pl.DeviceIdType.MESH)
    pl.semaphore_wait(barrier, len(partners))


def project_kernel(
    enc_hbm, kw_hbm, vw_hbm, q_hbm, g_hbm,
    kv_ref, w_hbm, qg_hbm,
    enc, wfull, qg, acc,
    load_sem, enc_sem, wout_sem, qgout_sem,
    zs, zr, qs, qr, xs, xr, ss, sr, sqs, sqr,
):
    e = lax.axis_index("enc")
    x = lax.axis_index("dec")
    nz, nx = 8, 4
    z, c = e // 2, e % 2
    other = e + 1 - 2 * c
    z_up, z_down = lax.rem(z + 1, nz) * 2 + c, lax.rem(z + nz - 1, nz) * 2 + c
    x_up, x_down = lax.rem(x + 1, nx), lax.rem(x + nx - 1, nx)
    x_far = lax.rem(x + 2, nx)

    enc_load = pltpu.make_async_copy(enc_hbm, enc, enc_sem)
    loads = [
        pltpu.make_async_copy(kw_hbm, wfull.at[e, x, :, pl.ds(0, 512)], load_sem.at[0]),
        pltpu.make_async_copy(vw_hbm, wfull.at[e, x, :, pl.ds(512, 512)], load_sem.at[1]),
        pltpu.make_async_copy(q_hbm.at[0], qg.at[e, :, pl.ds(0, 512)], load_sem.at[2]),
        pltpu.make_async_copy(g_hbm.at[0], qg.at[e, :, pl.ds(512, 512)], load_sem.at[3]),
    ]
    for load in loads:
        load.start()
    enc_load.start()
    greet([{"enc": z_up}, {"enc": z_down}, {"dec": x_up}, {"dec": x_down}, {"enc": other}])
    for load in loads:
        load.wait()

    def block_of(k):
        half = (k + 1) // 2
        offset = jnp.where(k % 2 == 1, -half, half)
        return lax.rem(z + offset + nz, nz) * 2 + c

    def z_copy(b, slot, up):
        return remote(wfull.at[b, x], wfull.at[b, x], zs.at[slot], zr.at[slot],
                      enc=z_up if up else z_down)

    def q_copy(b, slot, up):
        return remote(qg.at[b], qg.at[b], qs.at[slot], qr.at[slot], enc=z_up if up else z_down)

    def x_copies(k):
        b = block_of(k)
        return (
            remote(wfull.at[b, x], wfull.at[b, x], xs.at[k, 0], xr.at[k, 0], dec=x_up),
            remote(wfull.at[b, x], wfull.at[b, x], xs.at[k, 1], xr.at[k, 1], dec=x_down),
            remote(wfull.at[b, x_down, pl.ds(0, 32)], wfull.at[b, x_down, pl.ds(0, 32)],
                   xs.at[k, 2], xr.at[k, 2], dec=x_up),
            remote(wfull.at[b, x_up, pl.ds(32, 32)], wfull.at[b, x_up, pl.ds(32, 32)],
                   xs.at[k, 3], xr.at[k, 3], dec=x_down),
        )

    def s_copies(k):
        b = block_of(k)
        return (
            remote(wfull.at[b], wfull.at[b], ss.at[k], sr.at[k], enc=other),
            remote(qg.at[b], qg.at[b], sqs.at[k], sqr.at[k], enc=other),
        )

    def out_copy(b):
        return pltpu.make_async_copy(wfull.at[b], w_hbm.at[b], wout_sem.at[b])

    def qg_out(b):
        return pltpu.make_async_copy(qg.at[b], qg_hbm.at[b], qgout_sem.at[b])

    def multiply(b):
        weights = wfull[b].reshape(256, 1024)
        rows = enc[:, pl.ds(pl.multiple_of(b * 256, 256), 256)]
        acc[...] += jnp.dot(rows, weights, preferred_element_type=F32)

    z_copy(e, 1, True).start()
    z_copy(e, 2, False).start()
    acc[...] = jnp.zeros_like(acc)

    def step(k, _):
        odd = k % 2 == 1

        @pl.when(k < nz)
        def _():
            b = block_of(k)

            @pl.when(k > 0)
            def _():
                z_copy(b, k, True).wait_recv()

            @pl.when(jnp.logical_and(odd, k < 7))
            def _():
                z_copy(b, k + 2, True).start()

            @pl.when(jnp.logical_and(jnp.logical_and(k % 2 == 0, k > 0), k < 5))
            def _():
                z_copy(b, k + 2, False).start()

            one, two, _, _ = x_copies(k)
            one.start()
            two.start()

            @pl.when(k == 0)
            def _():
                q_copy(e, 1, True).start()
                q_copy(e, 2, False).start()

        @pl.when(jnp.logical_and(k > 0, k < nz + 1))
        def _():
            one, two, three, four = x_copies(k - 1)
            one.wait_recv()
            three.start()
            two.wait_recv()
            four.start()

        @pl.when(jnp.logical_and(k > 1, k < nz + 2))
        def _():
            _, _, three, four = x_copies(k - 2)
            b = block_of(k - 2)
            three.wait_recv()
            four.wait_recv()
            s_copies(k - 2)[0].start()
            out_copy(b).start()

            @pl.when(k == 2)
            def _():
                enc_load.wait()

            multiply(b)

            @pl.when(k > 2)
            def _():
                q_copy(b, k - 2, True).wait_recv()

            @pl.when(jnp.logical_and(odd, k < 9))
            def _():
                q_copy(b, k, True).start()

            @pl.when(jnp.logical_and(jnp.logical_and(k % 2 == 0, k > 2), k < 7))
            def _():
                q_copy(b, k, False).start()

            s_copies(k - 2)[1].start()
            qg_out(b).start()

        @pl.when(k > 2)
        def _():
            b = block_of(k - 3)
            mirror = b + 1 - 2 * c
            both = s_copies(k - 3)
            both[0].wait_recv()
            out_copy(mirror).start()
            multiply(mirror)
            both[1].wait_recv()
            qg_out(mirror).start()

        return 0

    lax.fori_loop(0, nz + 3, step, 0)
    kv_ref[...] = acc[...].astype(BF16)

    def finish(k, _):
        b = block_of(k)
        for copy in x_copies(k):
            copy.wait_send()
        for copy in s_copies(k):
            copy.wait_send()
        for which in (b, b + 1 - 2 * c):
            out_copy(which).wait()
            qg_out(which).wait()

        @pl.when(k > 0)
        def _():
            z_copy(b, k, True).wait_send()
            q_copy(b, k, True).wait_send()

        return 0

    lax.fori_loop(0, nz, finish, 0)


def project(encoded, key_weight, value_weight, queries, grad_context):
    any_spec = pl.BlockSpec(memory_space=pl.ANY)
    dma = pltpu.SemaphoreType.DMA
    return pl.pallas_call(
        project_kernel,
        out_shape=(
            jax.ShapeDtypeStruct((512, 1024), BF16),
            jax.ShapeDtypeStruct((16, 4, 64, 1024), BF16),
            jax.ShapeDtypeStruct((16, 64, 1024), BF16),
        ),
        in_specs=[any_spec] * 5,
        out_specs=(pl.BlockSpec(memory_space=pltpu.VMEM), any_spec, any_spec),
        scratch_shapes=[
            pltpu.VMEM((512, 4096), BF16),
            pltpu.VMEM((16, 4, 64, 1024), BF16),
            pltpu.VMEM((16, 64, 1024), BF16),
            pltpu.VMEM((512, 1024), F32),
            dma((4,)), dma, dma((16,)), dma((16,)),
            dma((8,)), dma((8,)), dma((8,)), dma((8,)),
            dma((8, 4)), dma((8, 4)),
            dma((8,)), dma((8,)), dma((8,)), dma((8,)),
        ],
        compiler_params=pltpu.CompilerParams(
            collective_id=1, has_side_effects=True, vmem_limit_bytes=40 * MIB
        ),
        cost_estimate=pl.CostEstimate(
            flops=2 * 512 * 4096 * 1024, bytes_accessed=30 * MIB, transcendentals=0
        ),
    )(encoded, key_weight, value_weight, queries, grad_context)


def head_mask(h, dtype):
    lane = lax.broadcasted_iota(jnp.int32, (1, WIDE), 1)
    inside = jnp.logical_and(lane >= h * HEAD_DIM, lane < (h + 1) * HEAD_DIM)
    return jnp.where(inside, 1.0, 0.0).astype(dtype)


def spread_heads(block):
    return jnp.concatenate([block * head_mask(h, BF16) for h in range(GROUP)], axis=0)


def attend_kernel(
    idx, kv_ref, qg_ref,
    gkv_ref, p_ref, gs_ref,
    s_scr, gc_scr, m_scr, l_scr, d_scr, mq_scr, lq_scr, dq_scr,
    out_st, in_st, fin_st,
    as_, ar, bs, br, own_sem,
):
    e = lax.axis_index("enc")
    n = 16

    def peer(i):
        return lax.rem(e + i, n)

    greet([{"enc": peer(i)} for i in range(1, n)])

    def first(p, _):
        j = jnp.maximum(idx[p], 0)
        rows = pl.ds(pl.multiple_of(p * 32, 32), 32)
        for g in range(2):
            cols = pl.ds(g * WIDE, WIDE)
            more = pl.ds(512 + g * WIDE, WIDE)
            q_wide = spread_heads(qg_ref[j, :, cols])
            g_wide = spread_heads(qg_ref[j, :, more])
            scores = lax.dot_general(kv_ref[rows, cols], q_wide, NT, preferred_element_type=F32)
            grads = lax.dot_general(kv_ref[rows, more], g_wide, NT, preferred_element_type=F32)
            s_scr[rows, cols] = scores
            gc_scr[rows, cols] = grads
            peak = jnp.max(scores, axis=0, keepdims=True)
            raised = jnp.exp(scores - peak)
            m_scr[pl.ds(p, 1), cols] = peak
            l_scr[pl.ds(p, 1), cols] = jnp.sum(raised, axis=0, keepdims=True)
            d_scr[pl.ds(p, 1), cols] = jnp.sum(raised * grads, axis=0, keepdims=True)
        return 0

    lax.fori_loop(0, n, first, 0)

    lane_q = lax.broadcasted_iota(jnp.int32, (n, 512), 0)
    peak = jnp.full((n, 512), LOW, F32)
    for p in range(n):
        peak = jnp.maximum(peak, jnp.where(lane_q == idx[p], m_scr[pl.ds(p, 1), :], LOW))
    mq_scr[...] = peak
    total = jnp.zeros((n, 512), F32)
    delta = jnp.zeros((n, 512), F32)
    for p in range(n):
        j = jnp.maximum(idx[p], 0)
        scale = jnp.exp(jnp.minimum(m_scr[pl.ds(p, 1), :] - mq_scr[pl.ds(j, 1), :], 0.0))
        mine = lane_q == idx[p]
        total = total + jnp.where(mine, scale * l_scr[pl.ds(p, 1), :], 0.0)
        delta = delta + jnp.where(mine, scale * d_scr[pl.ds(p, 1), :], 0.0)
    lq_scr[...] = total
    dq_scr[...] = delta
    for j in range(n):
        out_st[j, pl.ds(0, 1), :] = mq_scr[pl.ds(j, 1), :]
        out_st[j, pl.ds(1, 1), :] = lq_scr[pl.ds(j, 1), :]
        out_st[j, pl.ds(2, 1), :] = dq_scr[pl.ds(j, 1), :]
        out_st[j, pl.ds(3, 1), :] = dq_scr[pl.ds(j, 1), :]

    def to_owner(i):
        return remote(out_st.at[peer(i)], in_st.at[e], as_.at[i], ar.at[i], enc=peer(i))

    def from_owner(i):
        return remote(fin_st.at[e], fin_st.at[e], bs.at[i], br.at[i], enc=peer(i))

    own = pltpu.make_async_copy(out_st.at[e], in_st.at[e], own_sem)
    own.start()
    for i in range(1, n):
        to_owner(i).start()
    own.wait()
    for i in range(1, n):
        to_owner(i).wait_recv()

    peak = in_st[0, pl.ds(0, 1), :]
    for i in range(1, n):
        peak = jnp.maximum(peak, in_st[i, pl.ds(0, 1), :])
    total = jnp.zeros((1, 512), F32)
    delta = jnp.zeros((1, 512), F32)
    for i in range(n):
        scale = jnp.exp(in_st[i, pl.ds(0, 1), :] - peak)
        total = total + scale * in_st[i, pl.ds(1, 1), :]
        delta = delta + scale * in_st[i, pl.ds(2, 1), :]
    inverse = 1.0 / total
    fin_st[e, pl.ds(0, 1), :] = peak
    fin_st[e, pl.ds(1, 1), :] = inverse
    fin_st[e, pl.ds(2, 1), :] = delta * inverse
    fin_st[e, pl.ds(3, 1), :] = inverse
    for i in range(1, n):
        from_owner(i).start()
    for i in range(1, n):
        from_owner(i).wait_recv()

    def second(p, _):
        j = jnp.maximum(idx[p], 0)
        live = jnp.where(idx[p] >= 0, 1.0, 0.0)
        rows = pl.ds(pl.multiple_of(p * 32, 32), 32)
        for g in range(2):
            cols = pl.ds(g * WIDE, WIDE)
            more = pl.ds(512 + g * WIDE, WIDE)
            peak = fin_st[j, pl.ds(0, 1), cols]
            inverse = fin_st[j, pl.ds(1, 1), cols] * live
            delta = fin_st[j, pl.ds(2, 1), cols]
            chances = jnp.exp(jnp.minimum(s_scr[rows, cols] - peak, 0.0)) * inverse
            low = chances.astype(BF16)
            slope = (chances * (gc_scr[rows, cols] - delta)).astype(BF16)
            p_ref[rows, cols] = low
            gs_ref[rows, cols] = slope
            q_wide = spread_heads(qg_ref[j, :, cols])
            g_wide = spread_heads(qg_ref[j, :, more])
            gkv_ref[rows, cols] = jnp.dot(slope, q_wide, preferred_element_type=F32).astype(BF16)
            gkv_ref[rows, more] = jnp.dot(low, g_wide, preferred_element_type=F32).astype(BF16)
        return 0

    lax.fori_loop(0, n, second, 0)
    for i in range(1, n):
        to_owner(i).wait_send()
        from_owner(i).wait_send()


def attend(idx, kv, qg):
    vmem = pl.BlockSpec(memory_space=pltpu.VMEM)
    dma = pltpu.SemaphoreType.DMA
    return pl.pallas_call(
        attend_kernel,
        out_shape=(
            jax.ShapeDtypeStruct((512, 1024), BF16),
            jax.ShapeDtypeStruct((512, 512), BF16),
            jax.ShapeDtypeStruct((512, 512), BF16),
        ),
        in_specs=[pl.BlockSpec(memory_space=pltpu.SMEM), vmem, vmem],
        out_specs=(vmem, vmem, vmem),
        scratch_shapes=[pltpu.VMEM((512, 512), F32)] * 2
        + [pltpu.VMEM((16, 512), F32)] * 6
        + [pltpu.VMEM((16, 4, 512), F32)] * 3
        + [dma((16,))] * 4
        + [dma],
        compiler_params=pltpu.CompilerParams(
            collective_id=2, has_side_effects=True, vmem_limit_bytes=32 * MIB
        ),
        cost_estimate=pl.CostEstimate(
            flops=2 * 512 * 4096 * 512, bytes_accessed=8 * MIB, transcendentals=0
        ),
    )(idx, kv, qg)


def sums_kernel(idx, kv_ref, p_ref, gs_ref, out_ref, acc):
    acc[...] = jnp.zeros_like(acc)

    def step(p, _):
        j = jnp.maximum(idx[p], 0)
        rows = pl.ds(pl.multiple_of(p * 32, 32), 32)
        for g in range(2):
            cols = pl.ds(g * WIDE, WIDE)
            more = pl.ds(512 + g * WIDE, WIDE)
            for left, right, put in ((p_ref, more, cols), (gs_ref, cols, more)):
                square = lax.dot_general(
                    left[rows, cols], kv_ref[rows, right], TN, preferred_element_type=F32
                )
                part = square[0:HEAD_DIM] * head_mask(0, F32)
                for h in range(1, GROUP):
                    part = part + square[h * HEAD_DIM:(h + 1) * HEAD_DIM] * head_mask(h, F32)
                acc[j, :, put] += part
        return 0

    lax.fori_loop(0, 16, step, 0)
    out_ref[...] = acc[...].astype(BF16)


def sums(idx, kv, chances, slopes):
    vmem = pl.BlockSpec(memory_space=pltpu.VMEM)
    return pl.pallas_call(
        sums_kernel,
        out_shape=jax.ShapeDtypeStruct((16, 64, 1024), BF16),
        in_specs=[pl.BlockSpec(memory_space=pltpu.SMEM), vmem, vmem, vmem],
        out_specs=vmem,
        scratch_shapes=[pltpu.VMEM((16, 64, 1024), F32)],
        compiler_params=pltpu.CompilerParams(vmem_limit_bytes=32 * MIB),
        cost_estimate=pl.CostEstimate(
            flops=2 * 512 * 4096 * 512, bytes_accessed=8 * MIB, transcendentals=0
        ),
    )(idx, kv, chances, slopes)


def gradient_kernel(
    gkv_ref, w_hbm, out_hbm,
    wbuf, sbuf, rbuf, own, obuf,
    w_sem, rs, rr, gs, gr, fs, fr, out_sem,
):
    m = lax.axis_index("mp")
    right, left, far = lax.rem(m + 1, 4), lax.rem(m + 3, 4), lax.rem(m + 2, 4)
    sides = (right, left)

    def w_load(u, i):
        rows = pl.ds(pl.multiple_of(u * 1024 + i * 256, 256), 256)
        return pltpu.make_async_copy(w_hbm.at[rows], wbuf.at[rows], w_sem.at[u, i])

    order = [(far, 0), (far, 2), (far, 1), (far, 3), (right, 2), (left, 0), (right, 3), (left, 1),
             (right, 0), (left, 2), (right, 1), (left, 3), (m, 0), (m, 1), (m, 2), (m, 3)]
    for u, i in order:
        w_load(u, i).start()
    greet([{"mp": right}, {"mp": left}])

    def partial(u, i):
        w_load(u, i).wait()
        rows = pl.ds(pl.multiple_of(u * 1024 + i * 256, 256), 256)
        return lax.dot_general(gkv_ref[...], wbuf[rows, :], NT, preferred_element_type=F32)

    def reduce_copy(stage, side, k):
        return remote(sbuf.at[stage, side, k], rbuf.at[stage, side, k],
                      rs.at[stage, side, k], rr.at[stage, side, k], mp=sides[side])

    plan = (((far, 0), (far, 2)), ((right, 2), (left, 0)), ((right, 0), (left, 2)))
    for stage in range(3):

        def send(k, _, stage=stage):
            for side in range(2):
                u, base = plan[stage][side]
                term = partial(u, base + k).astype(BF16)
                if stage == 2:
                    reduce_copy(0, side, k).wait_recv()
                    term = (term.astype(F32) + rbuf[0, side, k].astype(F32)).astype(BF16)
                sbuf[stage, side, k] = term
                reduce_copy(stage, side, k).start()
            return 0

        lax.fori_loop(0, 2, send, 0)

    def mine(i, _):
        own[i] = partial(m, i).astype(BF16)
        return 0

    lax.fori_loop(0, 4, mine, 0)

    def gather_copy(u, i, side):
        return remote(obuf.at[u, i], obuf.at[u, i], gs.at[side, i], gr.at[side, i], mp=sides[side])

    def pass_on(u, k, side):
        i = 2 * side + k
        return remote(obuf.at[u, i], obuf.at[u, i], fs.at[side, k], fr.at[side, k], mp=sides[side])

    def write_out(u, i):
        cols = pl.ds(pl.multiple_of(u * 1024 + i * 256, 256), 256)
        return pltpu.make_async_copy(obuf.at[u, i], out_hbm.at[:, cols], out_sem.at[u, i])

    def total(k, _):
        for half in range(2):
            i = 2 * half + k
            reduce_copy(2, half, k).wait_recv()
            reduce_copy(1, 1 - half, k).wait_recv()
            value = own[i].astype(F32) + rbuf[2, half, k].astype(F32)
            value = value + rbuf[1, 1 - half, k].astype(F32)
            obuf[m, i] = value.astype(BF16)
            gather_copy(m, i, half).start()
            gather_copy(m, i, 1 - half).start()
            write_out(m, i).start()
        return 0

    lax.fori_loop(0, 2, total, 0)

    def forward(k, _):
        gather_copy(left, k, 0).wait_recv()
        pass_on(left, k, 0).start()
        write_out(left, k).start()
        gather_copy(right, 2 + k, 1).wait_recv()
        pass_on(right, k, 1).start()
        write_out(right, 2 + k).start()
        return 0

    lax.fori_loop(0, 2, forward, 0)

    def rest(k, _):
        gather_copy(left, 2 + k, 0).wait_recv()
        write_out(left, 2 + k).start()
        gather_copy(right, k, 1).wait_recv()
        write_out(right, k).start()
        return 0

    lax.fori_loop(0, 2, rest, 0)

    def last(k, _):
        pass_on(far, k, 0).wait_recv()
        write_out(far, k).start()
        pass_on(far, k, 1).wait_recv()
        write_out(far, 2 + k).start()
        return 0

    lax.fori_loop(0, 2, last, 0)

    def finish(k, _):
        for side in range(2):
            for stage in range(3):
                reduce_copy(stage, side, k).wait_send()
            gather_copy(m, k, side).wait_send()
            gather_copy(m, 2 + k, side).wait_send()
            pass_on(left if side == 0 else right, k, side).wait_send()
        for u in range(4):
            write_out(u, k).wait()
            write_out(u, 2 + k).wait()
        return 0

    lax.fori_loop(0, 2, finish, 0)


def gradient(gkv, weights):
    dma = pltpu.SemaphoreType.DMA
    any_spec = pl.BlockSpec(memory_space=pl.ANY)
    return pl.pallas_call(
        gradient_kernel,
        out_shape=jax.ShapeDtypeStruct((512, 4096), BF16),
        in_specs=[pl.BlockSpec(memory_space=pltpu.VMEM), any_spec],
        out_specs=any_spec,
        scratch_shapes=[
            pltpu.VMEM((4096, 1024), BF16),
            pltpu.VMEM((3, 2, 2, 512, 256), BF16),
            pltpu.VMEM((3, 2, 2, 512, 256), BF16),
            pltpu.VMEM((4, 512, 256), BF16),
            pltpu.VMEM((4, 4, 512, 256), BF16),
            dma((4, 4)),
            dma((3, 2, 2)), dma((3, 2, 2)),
            dma((2, 4)), dma((2, 4)),
            dma((2, 2)), dma((2, 2)),
            dma((4, 4)),
        ],
        compiler_params=pltpu.CompilerParams(
            collective_id=3, has_side_effects=True, vmem_limit_bytes=44 * MIB
        ),
        cost_estimate=pl.CostEstimate(
            flops=60 * 2 * 512 * 4096 * 1024, bytes_accessed=30 * MIB, transcendentals=0
        ),
    )(gkv, weights)


def on_device(encoded, owner, key_weight, value_weight, queries, grad_context):
    dec_count = lax.axis_size("dec")
    slots, length, width = encoded.shape
    idx = jnp.where(owner >= 0, owner // dec_count, -1)
    kv, weights, qg = project(
        encoded.reshape(slots * length, width), key_weight, value_weight, queries, grad_context
    )
    gkv, chances, slopes = attend(idx, kv, qg)
    parts = sums(idx, kv, chances, slopes)
    summed = lax.psum_scatter(parts, "enc", scatter_dimension=0, tiled=True)
    grad_encoded = gradient(gkv, weights.reshape(width, 1024))
    context = summed[:, :, :512]
    grad_queries = summed[:, :, 512:]
    return context, grad_queries, grad_encoded.reshape(encoded.shape)


def solution(mesh):
    rows = P(("enc", "dec"), None, None)
    cut = P(("enc", "dec"), None, "mp")
    weight = P(("enc", "dec"), "mp")
    return jax.shard_map(
        on_device,
        mesh=mesh,
        in_specs=(rows, P(("enc", "dec")), weight, weight, cut, cut),
        out_specs=(cut, cut, rows),
        check_vma=False,
    )
```

time: 365 us -> 187 us (0.51)
  waiting for transfers between devices: 213 us -> 0.02 us
  Pallas kernels: 0 us -> 158 us
  blocking collectives: 55.8 us -> 0 us
  matrix products: 27.7 us -> 0 us
  local copies, waits for them, and re-layouts: 30.5 us -> 13.7 us
  starting transfers between devices: 15.2 us -> 0.04 us
  other arithmetic: 7.85 us -> 0.66 us
    pallas_call x0 -> x4, Pallas kernels: none -> 158 us  [the longest x1 73.5 us: gradient(): pl.pallas_call(gradient_kernel, out_shape=jax.ShapeDtypeStruct((512, 4096...]
    psum x1 -> x0, waiting for transfers between devices: 88 us -> none  [on_device(): grad_flat = lax.psum(partial_sum.astype(jnp.bfloat16), 'mp')]
    all_gather x1 -> x0, waiting for transfers between devices: 76.8 us -> none  [on_device(): lax.all_gather(local_pair, ('enc', 'dec'), axis=0, tiled=True)]
    all_to_all x1 -> x0, blocking collectives: 55.8 us -> none  [on_device(): lax.all_to_all(returning, 'enc', split_axis=0, concat_axis=0, tiled=True)]
    all_to_all x2 -> x0, waiting for transfers between devices: 48.1 us -> none  [the longest x1 48.1 us: on_device(): lax.all_to_all(outgoing, 'enc', split_axis=0, concat_axis=0, tiled=True)]
    dot_general x9 -> x0, matrix products: 26.9 us -> none  [the longest x1 10.3 us: on_device(): lax.dot_general(grad_pair, lax.all_gather(local_pair, ('enc', 'dec'), axi...]
    all_to_all x2 -> x0, starting transfers between devices: 14.9 us -> none  [the longest x1 9.98 us: on_device(): lax.all_to_all(live_slots, 'enc', split_axis=0, concat_axis=0, tiled=True)]
    concatenate x2 -> x0, local copies, waits for them, and re-layouts: 6.2 us -> none  [on_device(): jnp.concatenate([grad_key.reshape(key_count, head_width), grad_value.resh...]
  transfers between devices with their start and end apart: 4 -> 1, of which waited for: 3 -> 0; matrix products, arithmetic and copies ran while one was open for 6% -> 0% of each run, Pallas kernels for 0% -> 39%
where the time goes in v1:
time: 187 us
  Pallas kernels  158 us (84%)
  between operations  14.1 us (8%)
  local copies, waits for them, and re-layouts  13.7 us (7%)
    pallas_call x1, Pallas kernels, gradient(): pl.pallas_call(gradient_kernel, out_shape=jax.ShapeDtypeStruct((512, 4096...  73.5 us
    pallas_call x1, Pallas kernels, project(): pl.pallas_call(project_kernel, out_shape=(jax.ShapeDtypeStruct((512, 1024...  51 us
    pallas_call x1, Pallas kernels, attend(): pl.pallas_call(attend_kernel, out_shape=(jax.ShapeDtypeStruct((512, 1024)...  26.1 us
    unnamed x13, local copies, waits for them, and re-layouts  12.2 us
    pallas_call x1, Pallas kernels, sums(): pl.pallas_call(sums_kernel, out_shape=jax.ShapeDtypeStruct((16, 64, 1024)...  7.66 us
  transfers between devices with their start and end apart: 1, of which 0 were waited for; matrix products, arithmetic and copies ran while one was open for 0% of the time, Pallas kernels for 39%

profile of v1, /device:TPU:1, one launch (start us, length us, event | category | flops | bytes accessed | tf_op | source)
XLA Modules:
  0.0 186.8 jit_solution(13167784614260705894)
XLA Ops:
  7.2 0.0 reduce-scatter.2.cloned.1.call-start
  7.2 0.7 compare_select_fusion.idx
  7.9 0.0 copy-start.1
  7.9 2.2 %copy-done.1 = bf16[16,32,4096]{2,1,0:T(8,128)(2,1)S(1)} copy-done((bf16[16,32,4096]{2,1,0:T(8,128)(2,1)S(1)}, bf16[16,32,4096]{2,1,0:T(8,128)(2,1)}, u32[]{:S(2)}) %copy-start.1) | copy-done | bytes 4194328
  10.1 0.0 copy-start.2
  10.1 0.8 copy-done.2
  10.9 0.0 copy-start.3
  10.9 0.8 copy-done.3
  11.7 0.0 copy-start.4
  11.7 0.8 copy-done.4
  12.6 0.0 copy-start.5
  12.6 0.8 copy-done.5
  13.4 51.0 %shard_map.85 = (bf16[512,1024]{1,0:T(8,128)(2,1)S(1)}, bf16[16,4,64,1024]{3,2,1,0:T(8,128)(2,1)}, bf16[16,64,1024]{2,1,0:T(8,128)(2,1)S(1)}) custom-call(bf16[512,4096]{1,0:T(8,128)(2,1)S(1)} %bitcast.4, bf16[64,512]{1,0:T(8,128)(2,1)S(1)} %copy-done.2, bf16[64,512]{1,0:T(8,128)(2,1)S(1)} %copy-done.3, bf16[1,64,512]{2,1,0:T(8,128)(2,1)S(1)} %copy-done.4, ...), custom_call_target="tpu_custom_call" | custom-call | flops 4294967296 | bytes 31457280 | tf_op jit(solution)/shard_map/pallas_call | solution.py:220
  64.4 26.1 %shard_map.86 = (bf16[512,1024]{1,0:T(8,128)(2,1)S(1)}, bf16[512,512]{1,0:T(8,128)(2,1)S(1)}, bf16[512,512]{1,0:T(8,128)(2,1)S(1)}) custom-call(s32[16]{0:T(128)S(1)} %compare_select_fusion.idx, bf16[512,1024]{1,0:T(8,128)(2,1)S(1)} %get-tuple-element.9.kv_ref, bf16[16,64,1024]{2,1,0:T(8,128)(2,1)S(1)} %get-tuple-element.10.qg_ref), custom_call_target="tpu_custom_call" | custom-call | flops 2147483648 | bytes 8388608 | tf_op jit(solution)/shard_map/pallas_call | solution.py:378
  90.6 7.7 %shard_map.87 = bf16[16,64,1024]{2,1,0:T(8,128)(2,1)} custom-call(s32[16]{0:T(128)S(1)} %compare_select_fusion.idx, bf16[512,1024]{1,0:T(8,128)(2,1)S(1)} %get-tuple-element.9.kv_ref, bf16[512,512]{1,0:T(8,128)(2,1)S(1)} %get-tuple-element.11.p_ref, bf16[512,512]{1,0:T(8,128)(2,1)S(1)} %get-tuple-element.12.gs_ref), custom_call_target="tpu_custom_call" | custom-call | flops 2147483648 | bytes 8388608 | tf_op jit(solution)/shard_map/pallas_call | solution.py:426
  98.2 0.0 reduce-scatter.2.cloned.1.call-update
  98.3 73.5 %shard_map.88 = bf16[512,4096]{1,0:T(8,128)(2,1)S(1)} custom-call(bf16[512,1024]{1,0:T(8,128)(2,1)S(1)} %get-tuple-element.13.gkv_ref, bf16[4096,1024]{1,0:T(8,128)(2,1)} %bitcast.5), custom_call_target="tpu_custom_call" | custom-call | flops 257698037760 | bytes 31457280 | tf_op jit(solution)/shard_map/pallas_call | solution.py:562
  171.8 0.0 copy-start
  171.8 1.9 %copy-done = bf16[512,4096]{1,0:T(8,128)(2,1)} copy-done((bf16[512,4096]{1,0:T(8,128)(2,1)}, bf16[512,4096]{1,0:T(8,128)(2,1)S(1)}, u32[]{:S(2)}) %copy-start) | copy-done | bytes 4194328
  173.7 0.0 reduce-scatter.2.cloned.1.call-done
  173.7 1.5 fusion
  175.3 4.7 %copy.10 = bf16[16,32,4096]{2,1,0:T(8,128)(2,1)} copy(bf16[16,32,4096]{2,1,0:T(8,128)(2,1)} %bitcast.3) | data formatting | bytes 8388608
Async XLA Ops:
  7.2 166.6 %reduce-scatter.2.cloned.1.call-start = ((), (), s32[]{:S(2)}) async-start(), calls=%async_computation.1 | async-start | bytes 2228224 | tf_op jit(solution)/shard_map/reduce_scatter | solution.py:597
  7.9 2.2 %copy-start.1 = (bf16[16,32,4096]{2,1,0:T(8,128)(2,1)S(1)}, bf16[16,32,4096]{2,1,0:T(8,128)(2,1)}, u32[]{:S(2)}) copy-start(bf16[16,32,4096]{2,1,0:T(8,128)(2,1)} %param.6) | copy-start | bytes 12582916
  10.1 0.8 copy-start.2
  10.9 0.8 copy-start.3
  11.7 0.8 copy-start.4
  12.6 0.8 copy-start.5
  171.8 1.9 %copy-start = (bf16[512,4096]{1,0:T(8,128)(2,1)}, bf16[512,4096]{1,0:T(8,128)(2,1)S(1)}, u32[]{:S(2)}) copy-start(bf16[512,4096]{1,0:T(8,128)(2,1)S(1)} %shard_map.88) | copy-start | bytes 12582916
Sparse Core Ops, SparseCore 0:
  98.4 54.8 reduce-scatter.1

commit v2 on v1

--- a/solution.py
+++ b/solution.py
@@ -215,7 +215,7 @@
 
 
 def project(encoded, key_weight, value_weight, queries, grad_context):
-    any_spec = pl.BlockSpec(memory_space=pl.ANY)
+    any_spec = pl.BlockSpec(memory_space=pltpu.HBM)
     dma = pltpu.SemaphoreType.DMA
     return pl.pallas_call(
         project_kernel,
@@ -225,7 +225,11 @@
             jax.ShapeDtypeStruct((16, 64, 1024), BF16),
         ),
         in_specs=[any_spec] * 5,
-        out_specs=(pl.BlockSpec(memory_space=pltpu.VMEM), any_spec, any_spec),
+        out_specs=(
+            pl.BlockSpec(memory_space=pltpu.VMEM),
+            any_spec,
+            pl.BlockSpec(memory_space=pl.ANY),
+        ),
         scratch_shapes=[
             pltpu.VMEM((512, 4096), BF16),
             pltpu.VMEM((16, 4, 64, 1024), BF16),
@@ -237,7 +241,7 @@
             dma((8,)), dma((8,)), dma((8,)), dma((8,)),
         ],
         compiler_params=pltpu.CompilerParams(
-            collective_id=1, has_side_effects=True, vmem_limit_bytes=40 * MIB
+            collective_id=1, has_side_effects=True, vmem_limit_bytes=60 * MIB
         ),
         cost_estimate=pl.CostEstimate(
             flops=2 * 512 * 4096 * 1024, bytes_accessed=30 * MIB, transcendentals=0
@@ -289,7 +293,7 @@
             d_scr[pl.ds(p, 1), cols] = jnp.sum(raised * grads, axis=0, keepdims=True)
         return 0
 
-    lax.fori_loop(0, n, first, 0)
+    lax.fori_loop(0, n, first, 0, unroll=4)
 
     lane_q = lax.broadcasted_iota(jnp.int32, (n, 512), 0)
     peak = jnp.full((n, 512), LOW, F32)
@@ -366,7 +370,7 @@
             gkv_ref[rows, more] = jnp.dot(low, g_wide, preferred_element_type=F32).astype(BF16)
         return 0
 
-    lax.fori_loop(0, n, second, 0)
+    lax.fori_loop(0, n, second, 0, unroll=4)
     for i in range(1, n):
         to_owner(i).wait_send()
         from_owner(i).wait_send()
@@ -398,74 +402,67 @@
     )(idx, kv, qg)
 
 
-def sums_kernel(idx, kv_ref, p_ref, gs_ref, out_ref, acc):
-    acc[...] = jnp.zeros_like(acc)
-
-    def step(p, _):
-        j = jnp.maximum(idx[p], 0)
-        rows = pl.ds(pl.multiple_of(p * 32, 32), 32)
+def gradient_kernel(
+    gkv_ref, w_hbm, rowq, kv_ref, p_ref, slope_ref,
+    obuf, ctx_ref, gq_ref,
+    wbuf, sbuf, rbuf, own, parts, arrived,
+    w_sem, rs, rr, gs, gr, fs, fr, ps, pr, part_sem,
+):
+    n = 16
+    e = lax.axis_index("enc")
+    m = lax.axis_index("mp")
+    right, left, far = lax.rem(m + 1, 4), lax.rem(m + 3, 4), lax.rem(m + 2, 4)
+    sides = (right, left)
+
+    def w_load(u, i):
+        rows = pl.ds(pl.multiple_of(u * 1024 + i * 256, 256), 256)
+        return pltpu.make_async_copy(w_hbm.at[rows], wbuf.at[rows], w_sem.at[u, i])
+
+    order = [(far, 0), (far, 2), (far, 1), (far, 3), (right, 2), (left, 0), (right, 3), (left, 1),
+             (right, 0), (left, 2), (right, 1), (left, 3), (m, 0), (m, 1), (m, 2), (m, 3)]
+    for u, i in order:
+        w_load(u, i).start()
+    greet([{"mp": right}, {"mp": left}] + [{"enc": lax.rem(e + i, n)} for i in range(1, n)])
+
+    def partial(u, i):
+        w_load(u, i).wait()
+        rows = pl.ds(pl.multiple_of(u * 1024 + i * 256, 256), 256)
+        return lax.dot_general(gkv_ref[...], wbuf[rows, :], NT, preferred_element_type=F32)
+
+    def reduce_copy(stage, side, k):
+        return remote(sbuf.at[stage, side, k], rbuf.at[stage, side, k],
+                      rs.at[stage, side, k], rr.at[stage, side, k], mp=sides[side])
+
+    def part_copy(i):
+        j = lax.rem(e + i, n)
+        return remote(parts.at[j], arrived.at[e], ps.at[i], pr.at[i], enc=j)
+
+    def part_of(i, _):
+        j = lax.rem(e + i, n)
+        mine = rowq[...] == j
         for g in range(2):
             cols = pl.ds(g * WIDE, WIDE)
             more = pl.ds(512 + g * WIDE, WIDE)
-            for left, right, put in ((p_ref, more, cols), (gs_ref, cols, more)):
+            for left_ref, other, put in ((p_ref, more, cols), (slope_ref, cols, more)):
                 square = lax.dot_general(
-                    left[rows, cols], kv_ref[rows, right], TN, preferred_element_type=F32
+                    jnp.where(mine, left_ref[:, cols], jnp.zeros((), BF16)), kv_ref[:, other], TN,
+                    preferred_element_type=F32,
                 )
                 part = square[0:HEAD_DIM] * head_mask(0, F32)
                 for h in range(1, GROUP):
                     part = part + square[h * HEAD_DIM:(h + 1) * HEAD_DIM] * head_mask(h, F32)
-                acc[j, :, put] += part
-        return 0
-
-    lax.fori_loop(0, 16, step, 0)
-    out_ref[...] = acc[...].astype(BF16)
-
-
-def sums(idx, kv, chances, slopes):
-    vmem = pl.BlockSpec(memory_space=pltpu.VMEM)
-    return pl.pallas_call(
-        sums_kernel,
-        out_shape=jax.ShapeDtypeStruct((16, 64, 1024), BF16),
-        in_specs=[pl.BlockSpec(memory_space=pltpu.SMEM), vmem, vmem, vmem],
-        out_specs=vmem,
-        scratch_shapes=[pltpu.VMEM((16, 64, 1024), F32)],
-        compiler_params=pltpu.CompilerParams(vmem_limit_bytes=32 * MIB),
-        cost_estimate=pl.CostEstimate(
-            flops=2 * 512 * 4096 * 512, bytes_accessed=8 * MIB, transcendentals=0
-        ),
-    )(idx, kv, chances, slopes)
-
-
-def gradient_kernel(
-    gkv_ref, w_hbm, out_hbm,
-    wbuf, sbuf, rbuf, own, obuf,
-    w_sem, rs, rr, gs, gr, fs, fr, out_sem,
-):
-    m = lax.axis_index("mp")
-    right, left, far = lax.rem(m + 1, 4), lax.rem(m + 3, 4), lax.rem(m + 2, 4)
-    sides = (right, left)
-
-    def w_load(u, i):
-        rows = pl.ds(pl.multiple_of(u * 1024 + i * 256, 256), 256)
-        return pltpu.make_async_copy(w_hbm.at[rows], wbuf.at[rows], w_sem.at[u, i])
-
-    order = [(far, 0), (far, 2), (far, 1), (far, 3), (right, 2), (left, 0), (right, 3), (left, 1),
-             (right, 0), (left, 2), (right, 1), (left, 3), (m, 0), (m, 1), (m, 2), (m, 3)]
-    for u, i in order:
-        w_load(u, i).start()
-    greet([{"mp": right}, {"mp": left}])
-
-    def partial(u, i):
-        w_load(u, i).wait()
-        rows = pl.ds(pl.multiple_of(u * 1024 + i * 256, 256), 256)
-        return lax.dot_general(gkv_ref[...], wbuf[rows, :], NT, preferred_element_type=F32)
-
-    def reduce_copy(stage, side, k):
-        return remote(sbuf.at[stage, side, k], rbuf.at[stage, side, k],
-                      rs.at[stage, side, k], rr.at[stage, side, k], mp=sides[side])
+                parts[j, :, put] = part.astype(BF16)
+
+        @pl.when(i < n)
+        def _():
+            part_copy(i).start()
+
+        return 0
 
     plan = (((far, 0), (far, 2)), ((right, 2), (left, 0)), ((right, 0), (left, 2)))
     for stage in range(3):
+        if stage == 2:
+            lax.fori_loop(1, n + 1, part_of, 0)
 
         def send(k, _, stage=stage):
             for side in range(2):
@@ -493,10 +490,6 @@
         i = 2 * side + k
         return remote(obuf.at[u, i], obuf.at[u, i], fs.at[side, k], fr.at[side, k], mp=sides[side])
 
-    def write_out(u, i):
-        cols = pl.ds(pl.multiple_of(u * 1024 + i * 256, 256), 256)
-        return pltpu.make_async_copy(obuf.at[u, i], out_hbm.at[:, cols], out_sem.at[u, i])
-
     def total(k, _):
         for half in range(2):
             i = 2 * half + k
@@ -507,7 +500,6 @@
             obuf[m, i] = value.astype(BF16)
             gather_copy(m, i, half).start()
             gather_copy(m, i, 1 - half).start()
-            write_out(m, i).start()
         return 0
 
     lax.fori_loop(0, 2, total, 0)
@@ -515,31 +507,40 @@
     def forward(k, _):
         gather_copy(left, k, 0).wait_recv()
         pass_on(left, k, 0).start()
-        write_out(left, k).start()
         gather_copy(right, 2 + k, 1).wait_recv()
         pass_on(right, k, 1).start()
-        write_out(right, 2 + k).start()
         return 0
 
     lax.fori_loop(0, 2, forward, 0)
 
     def rest(k, _):
         gather_copy(left, 2 + k, 0).wait_recv()
-        write_out(left, 2 + k).start()
         gather_copy(right, k, 1).wait_recv()
-        write_out(right, k).start()
         return 0
 
     lax.fori_loop(0, 2, rest, 0)
 
     def last(k, _):
         pass_on(far, k, 0).wait_recv()
-        write_out(far, k).start()
         pass_on(far, k, 1).wait_recv()
-        write_out(far, 2 + k).start()
         return 0
 
     lax.fori_loop(0, 2, last, 0)
+
+    def collect(i, _):
+        part_copy(i).wait_recv()
+        return 0
+
+    own_part = pltpu.make_async_copy(parts.at[e], arrived.at[e], part_sem)
+    own_part.start()
+    own_part.wait()
+    lax.fori_loop(1, n, collect, 0)
+    for half, put in enumerate((ctx_ref, gq_ref)):
+        cols = pl.ds(half * 512, 512)
+        put[...] = lax.fori_loop(
+            1, n, lambda i, so_far: so_far + arrived[i, :, cols].astype(F32),
+            arrived[0, :, cols].astype(F32),
+        ).astype(BF16)
 
     def finish(k, _):
         for side in range(2):
@@ -548,41 +549,73 @@
             gather_copy(m, k, side).wait_send()
             gather_copy(m, 2 + k, side).wait_send()
             pass_on(left if side == 0 else right, k, side).wait_send()
-        for u in range(4):
-            write_out(u, k).wait()
-            write_out(u, 2 + k).wait()
         return 0
 
     lax.fori_loop(0, 2, finish, 0)
 
-
-def gradient(gkv, weights):
+    def finish_parts(i, _):
+        part_copy(i).wait_send()
+        return 0
+
+    lax.fori_loop(1, n, finish_parts, 0)
+
+
+def gradient(gkv, weights, rowq, kv, chances, slopes):
     dma = pltpu.SemaphoreType.DMA
-    any_spec = pl.BlockSpec(memory_space=pl.ANY)
+    vmem = pl.BlockSpec(memory_space=pltpu.VMEM)
     return pl.pallas_call(
         gradient_kernel,
-        out_shape=jax.ShapeDtypeStruct((512, 4096), BF16),
-        in_specs=[pl.BlockSpec(memory_space=pltpu.VMEM), any_spec],
-        out_specs=any_spec,
+        out_shape=(
+            jax.ShapeDtypeStruct((4, 4, 512, 256), BF16),
+            jax.ShapeDtypeStruct((64, 512), BF16),
+            jax.ShapeDtypeStruct((64, 512), BF16),
+        ),
+        in_specs=[vmem, pl.BlockSpec(memory_space=pltpu.HBM), vmem, vmem, vmem, vmem],
+        out_specs=(vmem, vmem, vmem),
         scratch_shapes=[
             pltpu.VMEM((4096, 1024), BF16),
             pltpu.VMEM((3, 2, 2, 512, 256), BF16),
             pltpu.VMEM((3, 2, 2, 512, 256), BF16),
             pltpu.VMEM((4, 512, 256), BF16),
-            pltpu.VMEM((4, 4, 512, 256), BF16),
+            pltpu.VMEM((16, 64, 1024), BF16),
+            pltpu.VMEM((16, 64, 1024), BF16),
             dma((4, 4)),
             dma((3, 2, 2)), dma((3, 2, 2)),
             dma((2, 4)), dma((2, 4)),
             dma((2, 2)), dma((2, 2)),
-            dma((4, 4)),
+            dma((16,)), dma((16,)), dma,
         ],
         compiler_params=pltpu.CompilerParams(
             collective_id=3, has_side_effects=True, vmem_limit_bytes=44 * MIB
         ),
         cost_estimate=pl.CostEstimate(
-            flops=60 * 2 * 512 * 4096 * 1024, bytes_accessed=30 * MIB, transcendentals=0
-        ),
-    )(gkv, weights)
+            flops=2 * 512 * 4096 * 1024, bytes_accessed=30 * MIB, transcendentals=0
+        ),
+    )(gkv, weights, rowq, kv, chances, slopes)
+
+
+def place_kernel(pieces, out_hbm, sems):
+    copies = [
+        pltpu.make_async_copy(
+            pieces.at[i // 4, i % 4], out_hbm.at[:, pl.ds(i * 256, 256)], sems.at[i]
+        )
+        for i in range(16)
+    ]
+    for copy in copies:
+        copy.start()
+    for copy in copies:
+        copy.wait()
+
+
+def place(pieces):
+    return pl.pallas_call(
+        place_kernel,
+        out_shape=jax.ShapeDtypeStruct((512, 4096), BF16),
+        in_specs=[pl.BlockSpec(memory_space=pltpu.VMEM)],
+        out_specs=pl.BlockSpec(memory_space=pltpu.HBM),
+        scratch_shapes=[pltpu.SemaphoreType.DMA((16,))],
+        compiler_params=pltpu.CompilerParams(vmem_limit_bytes=16 * MIB),
+    )(pieces)
 
 
 def on_device(encoded, owner, key_weight, value_weight, queries, grad_context):
@@ -593,12 +626,12 @@
         encoded.reshape(slots * length, width), key_weight, value_weight, queries, grad_context
     )
     gkv, chances, slopes = attend(idx, kv, qg)
-    parts = sums(idx, kv, chances, slopes)
-    summed = lax.psum_scatter(parts, "enc", scatter_dimension=0, tiled=True)
-    grad_encoded = gradient(gkv, weights.reshape(width, 1024))
-    context = summed[:, :, :512]
-    grad_queries = summed[:, :, 512:]
-    return context, grad_queries, grad_encoded.reshape(encoded.shape)
+    rowq = jnp.repeat(idx, length).reshape(slots * length, 1)
+    pieces, context, grad_queries = gradient(
+        gkv, weights.reshape(width, 1024), rowq, kv, chances, slopes
+    )
+    grad_encoded = place(pieces).reshape(encoded.shape)
+    return context[None], grad_queries[None], grad_encoded
 
 
 def solution(mesh):

time: 187 us -> 160 us (0.86)
  between operations: 14.1 us -> 0.69 us
  local copies, waits for them, and re-layouts: 13.7 us -> 4.4 us
  Pallas kernels: 158 us -> 154 us
    unnamed x13 -> x8, local copies, waits for them, and re-layouts: 12.2 us -> 4.07 us
    pallas_call x1, Pallas kernels: 26.1 us -> 19.9 us  [attend(): pl.pallas_call(attend_kernel, out_shape=(jax.ShapeDtypeStruct((512, 1024)...]
    pallas_call x1, Pallas kernels: 51 us -> 53.5 us  [project(): pl.pallas_call(project_kernel, out_shape=(jax.ShapeDtypeStruct((512, 1024...]
  transfers between devices with their start and end apart: 1 -> 0, of which waited for: 0 -> 0; matrix products, arithmetic and copies ran while one was open for 0% -> 0% of each run, Pallas kernels for 39% -> 0%
where the time goes in v2:
time: 160 us
  Pallas kernels  154 us (96%)
  local copies, waits for them, and re-layouts  4.4 us (3%)
    pallas_call x1, Pallas kernels, gradient(): pl.pallas_call(gradient_kernel, out_shape=(jax.ShapeDtypeStruct((4, 4, 51...  78.4 us
    pallas_call x1, Pallas kernels, project(): pl.pallas_call(project_kernel, out_shape=(jax.ShapeDtypeStruct((512, 1024...  53.5 us
    pallas_call x1, Pallas kernels, attend(): pl.pallas_call(attend_kernel, out_shape=(jax.ShapeDtypeStruct((512, 1024)...  19.9 us
    unnamed x8, local copies, waits for them, and re-layouts  4.07 us

profile of v2, /device:TPU:1, one launch (start us, length us, event | category | flops | bytes accessed | tf_op | source)
XLA Modules:
  0.0 159.7 jit_solution(7037012594516122152)
XLA Ops:
  0.6 0.7 compare_select_fusion.idx
  1.3 0.1 broadcast_in_dim.11
  1.4 0.3 reshape_reshape.4.rowq
  1.6 53.5 %shard_map.85 = (bf16[512,1024]{1,0:T(8,128)(2,1)}, bf16[16,4,64,1024]{3,2,1,0:T(8,128)(2,1)}, bf16[16,64,1024]{2,1,0:T(8,128)(2,1)}) custom-call(bf16[512,4096]{1,0:T(8,128)(2,1)} %bitcast.8, bf16[64,512]{1,0:T(8,128)(2,1)} %kw_hbm.1, bf16[64,512]{1,0:T(8,128)(2,1)} %vw_hbm.1, bf16[1,64,512]{2,1,0:T(8,128)(2,1)} %q_hbm.1, bf16[1,64,512]{2,1,0:T(8,128)(2,1)} %g_hbm.1), custom_call_target="tpu_custom_call" | custom-call | flops 4294967296 | bytes 31457280 | tf_op jit(solution)/shard_map/pallas_call | solution.py:220
  55.2 0.0 copy-start
  55.2 1.6 copy-done
  56.8 0.0 copy-start.1
  56.8 1.2 copy-done.1
  58.0 0.0 copy-start.2
  58.0 19.9 %shard_map.86 = (bf16[512,1024]{1,0:T(8,128)(2,1)S(1)}, bf16[512,512]{1,0:T(8,128)(2,1)S(1)}, bf16[512,512]{1,0:T(8,128)(2,1)S(1)}) custom-call(s32[16]{0:T(128)S(1)} %compare_select_fusion.idx, bf16[512,1024]{1,0:T(8,128)(2,1)S(1)} %copy-done.1, bf16[16,64,1024]{2,1,0:T(8,128)(2,1)S(1)} %copy-done), custom_call_target="tpu_custom_call" | custom-call | flops 2147483648 | bytes 8388608 | tf_op jit(solution)/shard_map/pallas_call | solution.py:382
  77.9 0.0 copy-done.2
  77.9 78.4 %shard_map.87 = (bf16[4,4,512,256]{3,2,1,0:T(8,128)(2,1)S(1)}, bf16[64,512]{1,0:T(8,128)(2,1)S(1)}, bf16[64,512]{1,0:T(8,128)(2,1)S(1)}) custom-call(bf16[512,1024]{1,0:T(8,128)(2,1)S(1)} %get-tuple-element.14.gkv_ref, bf16[4096,1024]{1,0:T(8,128)(2,1)} %bitcast.9, s32[512,1]{1,0:T(8,128)S(1)} %reshape_reshape.4.rowq, bf16[512,1024]{1,0:T(8,128)(2,1)S(1)} %copy-done.2, ...), custom_call_target="tpu_custom_call" | custom-call | flops 4294967296 | bytes 31457280 | tf_op jit(solution)/shard_map/pallas_call | solution.py:566
  156.3 2.1 %shard_map.88 = bf16[512,4096]{1,0:T(8,128)(2,1)} custom-call(bf16[4,4,512,256]{3,2,1,0:T(8,128)(2,1)S(1)} %get-tuple-element.20.pieces), custom_call_target="tpu_custom_call" | custom-call | tf_op jit(solution)/shard_map/pallas_call | solution.py:611
  158.5 0.6 copy.12
  159.1 0.6 copy.13
Async XLA Ops:
  55.2 1.6 copy-start
  56.8 1.2 copy-start.1
  58.0 19.9 %copy-start.2 = (bf16[512,1024]{1,0:T(8,128)(2,1)S(1)}, bf16[512,1024]{1,0:T(8,128)(2,1)}, u32[]{:S(2)}) copy-start(bf16[512,1024]{1,0:T(8,128)(2,1)} %get-tuple-element.12.kv_ref) | copy-start | bytes 3145732

commit v3 on v2

v3 whole, which is shorter than its diff:
```python
import functools

import jax
import jax.numpy as jnp
from jax import lax
from jax.experimental import pallas as pl
from jax.experimental.pallas import tpu as pltpu
from jax.sharding import PartitionSpec as P

HEAD_DIM = 64
GROUP = 4
WIDE = GROUP * HEAD_DIM
LOW = -1e30
MIB = 1024 * 1024
BF16 = jnp.bfloat16
F32 = jnp.float32

NT = (((1,), (1,)), ((), ()))
TN = (((0,), (0,)), ((), ()))


def remote(src, dst, send_sem, recv_sem, **where):
    return pltpu.make_async_remote_copy(
        src_ref=src,
        dst_ref=dst,
        send_sem=send_sem,
        recv_sem=recv_sem,
        device_id=where,
        device_id_type=pl.DeviceIdType.MESH,
    )


def greet(partners):
    barrier = pltpu.get_barrier_semaphore()
    for where in partners:
        pl.semaphore_signal(barrier, inc=1, device_id=where, device_id_type=pl.DeviceIdType.MESH)
    pl.semaphore_wait(barrier, len(partners))


def head_mask(h, dtype):
    lane = lax.broadcasted_iota(jnp.int32, (1, WIDE), 1)
    inside = jnp.logical_and(lane >= h * HEAD_DIM, lane < (h + 1) * HEAD_DIM)
    return jnp.where(inside, 1.0, 0.0).astype(dtype)


def spread_heads(block):
    return jnp.concatenate([block * head_mask(h, BF16) for h in range(GROUP)], axis=0)


def whole_kernel(
    owner, enc_hbm, kw_hbm, vw_hbm, q_hbm, g_hbm,
    out_hbm, ctx_ref, gq_ref,
    obuf, enc, wfull, qg, acc, kv_ref, gkv_ref, p_ref, slope_ref,
    s_scr, gc_scr, m_scr, l_scr, d_scr, mq_scr, lq_scr, dq_scr, out_st, in_st, fin_st, rowq,
    sbuf, rbuf, own, parts, arrived,
    load_sem, enc_sem,
    zs, zr, vs, vr, qs, qr, xs, xr, ws, wr, ss, sr, sqs, sqr,
    as_, ar, bs, br, own_sem,
    rs, rr, gs, gr, fs, fr, ps, pr, part_sem, out_sem,
):
    e = lax.axis_index("enc")
    x = lax.axis_index("dec")
    m = lax.axis_index("mp")
    n, nz, nx, ny = 16, 8, 4, 4
    z, c = e // 2, e % 2
    other = e + 1 - 2 * c
    z_up, z_down = lax.rem(z + 1, nz) * 2 + c, lax.rem(z + nz - 1, nz) * 2 + c
    x_up, x_down = lax.rem(x + 1, nx), lax.rem(x + nx - 1, nx)
    right, left, far = lax.rem(m + 1, ny), lax.rem(m + 3, ny), lax.rem(m + 2, ny)
    sides = (right, left)

    def peer(i):
        return lax.rem(e + i, n)

    first_cols, last_cols = pl.ds(0, 768), pl.ds(768, 256)
    enc_load = pltpu.make_async_copy(enc_hbm, enc, enc_sem)
    loads = [
        pltpu.make_async_copy(kw_hbm, wfull.at[e, x, :, pl.ds(0, 512)], load_sem.at[0]),
        pltpu.make_async_copy(vw_hbm, wfull.at[e, x, :, pl.ds(512, 512)], load_sem.at[1]),
        pltpu.make_async_copy(q_hbm.at[0], qg.at[e, :, pl.ds(0, 512)], load_sem.at[2]),
        pltpu.make_async_copy(g_hbm.at[0], qg.at[e, :, pl.ds(512, 512)], load_sem.at[3]),
    ]
    for load in loads:
        load.start()
    enc_load.start()
    greet(
        [{"dec": x_up}, {"dec": x_down}, {"mp": right}, {"mp": left}]
        + [{"enc": peer(i)} for i in range(1, n)]
    )
    for load in loads:
        load.wait()

    def block_of(k):
        half = (k + 1) // 2
        offset = jnp.where(k % 2 == 1, -half, half)
        return lax.rem(z + offset + nz, nz) * 2 + c

    def z_copy(b, slot, where):
        part = wfull.at[b, x, :, first_cols]
        return remote(part, part, zs.at[slot], zr.at[slot], enc=where)

    def v_copy(b, slot, where):
        part = wfull.at[b, :, :, last_cols]
        return remote(part, part, vs.at[slot], vr.at[slot], enc=where)

    def q_copy(b, slot, where):
        return remote(qg.at[b], qg.at[b], qs.at[slot], qr.at[slot], enc=where)

    def x_four(b, cols, send, recv):
        whole = wfull.at[b, x, :, cols]
        low = wfull.at[b, x_down, pl.ds(0, 32), cols]
        high = wfull.at[b, x_up, pl.ds(32, 32), cols]
        return (
            remote(whole, whole, send(0), recv(0), dec=x_up),
            remote(whole, whole, send(1), recv(1), dec=x_down),
            remote(low, low, send(2), recv(2), dec=x_up),
            remote(high, high, send(3), recv(3), dec=x_down),
        )

    def x_copies(k):
        return x_four(block_of(k), first_cols, lambda i: xs.at[k, i], lambda i: xr.at[k, i])

    def w_copies():
        return x_four(e, last_cols, lambda i: ws.at[i], lambda i: wr.at[i])

    def s_copy(k):
        b = block_of(k)
        return remote(wfull.at[b], wfull.at[b], ss.at[k], sr.at[k], enc=other)

    def sq_copy(k):
        b = block_of(k)
        return remote(qg.at[b], qg.at[b], sqs.at[k], sqr.at[k], enc=other)

    def multiply(b):
        rows = enc[:, pl.ds(pl.multiple_of(b * 256, 256), 256)]
        acc[...] += jnp.dot(rows, wfull[b].reshape(256, 1024), preferred_element_type=F32)

    w_copies()[0].start()
    w_copies()[1].start()
    z_copy(e, 1, z_up).start()
    z_copy(e, 2, z_down).start()
    acc[...] = jnp.zeros_like(acc)

    def every(low, k, high):
        return jnp.logical_and(k >= low, k <= high)

    def step(k, _):
        odd = k % 2 == 1

        @pl.when(k < nz)
        def _():
            b = block_of(k)

            @pl.when(k > 0)
            def _():
                z_copy(b, k, z_up).wait_recv()

            @pl.when(jnp.logical_and(odd, k < 7))
            def _():
                z_copy(b, k + 2, z_up).start()

            @pl.when(jnp.logical_and(jnp.logical_not(odd), every(2, k, 4)))
            def _():
                z_copy(b, k + 2, z_down).start()

            one, two, _, _ = x_copies(k)
            one.start()
            two.start()

        @pl.when(k == 1)
        def _():
            one, two, three, four = w_copies()
            one.wait_recv()
            three.start()
            two.wait_recv()
            four.start()

        @pl.when(k == 2)
        def _():
            _, _, three, four = w_copies()
            three.wait_recv()
            four.wait_recv()
            v_copy(e, 1, z_up).start()
            v_copy(e, 2, z_down).start()
            q_copy(e, 1, z_up).start()
            q_copy(e, 2, z_down).start()

        @pl.when(every(2, k, nz + 1))
        def _():
            one, two, three, four = x_copies(k - 2)
            one.wait_recv()
            three.start()
            two.wait_recv()
            four.start()

        @pl.when(every(3, k, nz + 2))
        def _():
            at = k - 3
            b = block_of(at)

            @pl.when(at > 0)
            def _():
                v_copy(b, at, z_up).wait_recv()

            @pl.when(jnp.logical_and(at % 2 == 1, at < 5))
            def _():
                v_copy(b, at + 2, z_up).start()

            @pl.when(jnp.logical_and(at % 2 == 0, every(2, at, 4)))
            def _():
                v_copy(b, at + 2, z_down).start()

            @pl.when(at == 6)
            def _():
                v_copy(b, 7, z_down).start()

            _, _, three, four = x_copies(at)
            three.wait_recv()
            four.wait_recv()
            s_copy(at).start()

            @pl.when(at == 0)
            def _():
                enc_load.wait()

            multiply(b)

            @pl.when(at > 0)
            def _():
                q_copy(b, at, z_up).wait_recv()

            @pl.when(jnp.logical_and(at % 2 == 1, at < 7))
            def _():
                q_copy(b, at + 2, z_up).start()

            @pl.when(jnp.logical_and(at % 2 == 0, every(2, at, 4)))
            def _():
                q_copy(b, at + 2, z_down).start()

            sq_copy(at).start()

        @pl.when(k > 3)
        def _():
            s_copy(k - 4).wait_recv()
            multiply(block_of(k - 4) + 1 - 2 * c)
            sq_copy(k - 4).wait_recv()

        return 0

    lax.fori_loop(0, nz + 4, step, 0)
    kv_ref[...] = acc[...].astype(BF16)

    def question(p):
        held = owner[p]
        return jnp.where(held >= 0, held // nx, -1)

    def first(p, _):
        j = jnp.maximum(question(p), 0)
        rows = pl.ds(pl.multiple_of(p * 32, 32), 32)
        rowq[rows, :] = jnp.full((32, 1), question(p), jnp.int32)
        for g in range(2):
            cols = pl.ds(g * WIDE, WIDE)
            more = pl.ds(512 + g * WIDE, WIDE)
            q_wide = spread_heads(qg[j, :, cols])
            g_wide = spread_heads(qg[j, :, more])
            scores = lax.dot_general(kv_ref[rows, cols], q_wide, NT, preferred_element_type=F32)
            grads = lax.dot_general(kv_ref[rows, more], g_wide, NT, preferred_element_type=F32)
            s_scr[rows, cols] = scores
            gc_scr[rows, cols] = grads
            peak = jnp.max(scores, axis=0, keepdims=True)
            raised = jnp.exp(scores - peak)
            m_scr[pl.ds(p, 1), cols] = peak
            l_scr[pl.ds(p, 1), cols] = jnp.sum(raised, axis=0, keepdims=True)
            d_scr[pl.ds(p, 1), cols] = jnp.sum(raised * grads, axis=0, keepdims=True)
        return 0

    lax.fori_loop(0, n, first, 0, unroll=4)

    lane_q = lax.broadcasted_iota(jnp.int32, (n, 512), 0)
    peak = jnp.full((n, 512), LOW, F32)
    for p in range(n):
        peak = jnp.maximum(peak, jnp.where(lane_q == question(p), m_scr[pl.ds(p, 1), :], LOW))
    mq_scr[...] = peak
    total = jnp.zeros((n, 512), F32)
    delta = jnp.zeros((n, 512), F32)
    for p in range(n):
        j = jnp.maximum(question(p), 0)
        scale = jnp.exp(jnp.minimum(m_scr[pl.ds(p, 1), :] - mq_scr[pl.ds(j, 1), :], 0.0))
        mine = lane_q == question(p)
        total = total + jnp.where(mine, scale * l_scr[pl.ds(p, 1), :], 0.0)
        delta = delta + jnp.where(mine, scale * d_scr[pl.ds(p, 1), :], 0.0)
    lq_scr[...] = total
    dq_scr[...] = delta
    for j in range(n):
        out_st[j, pl.ds(0, 1), :] = mq_scr[pl.ds(j, 1), :]
        out_st[j, pl.ds(1, 1), :] = lq_scr[pl.ds(j, 1), :]
        out_st[j, pl.ds(2, 1), :] = dq_scr[pl.ds(j, 1), :]
        out_st[j, pl.ds(3, 1), :] = dq_scr[pl.ds(j, 1), :]

    def to_owner(i):
        return remote(out_st.at[peer(i)], in_st.at[e], as_.at[i], ar.at[i], enc=peer(i))

    def from_owner(i):
        return remote(fin_st.at[e], fin_st.at[e], bs.at[i], br.at[i], enc=peer(i))

    own_st = pltpu.make_async_copy(out_st.at[e], in_st.at[e], own_sem)
    own_st.start()
    for i in range(1, n):
        to_owner(i).start()
    own_st.wait()
    for i in range(1, n):
        to_owner(i).wait_recv()

    peak = in_st[0, pl.ds(0, 1), :]
    for i in range(1, n):
        peak = jnp.maximum(peak, in_st[i, pl.ds(0, 1), :])
    total = jnp.zeros((1, 512), F32)
    delta = jnp.zeros((1, 512), F32)
    for i in range(n):
        scale = jnp.exp(in_st[i, pl.ds(0, 1), :] - peak)
        total = total + scale * in_st[i, pl.ds(1, 1), :]
        delta = delta + scale * in_st[i, pl.ds(2, 1), :]
    inverse = 1.0 / total
    fin_st[e, pl.ds(0, 1), :] = peak
    fin_st[e, pl.ds(1, 1), :] = inverse
    fin_st[e, pl.ds(2, 1), :] = delta * inverse
    fin_st[e, pl.ds(3, 1), :] = inverse
    for i in range(1, n):
        from_owner(i).start()
    for i in range(1, n):
        from_owner(i).wait_recv()

    def second(p, _):
        j = jnp.maximum(question(p), 0)
        live = jnp.where(question(p) >= 0, 1.0, 0.0)
        rows = pl.ds(pl.multiple_of(p * 32, 32), 32)
        for g in range(2):
            cols = pl.ds(g * WIDE, WIDE)
            more = pl.ds(512 + g * WIDE, WIDE)
            peak = fin_st[j, pl.ds(0, 1), cols]
            inverse = fin_st[j, pl.ds(1, 1), cols] * live
            delta = fin_st[j, pl.ds(2, 1), cols]
            chances = jnp.exp(jnp.minimum(s_scr[rows, cols] - peak, 0.0)) * inverse
            low = chances.astype(BF16)
            slope = (chances * (gc_scr[rows, cols] - delta)).astype(BF16)
            p_ref[rows, cols] = low
            slope_ref[rows, cols] = slope
            q_wide = spread_heads(qg[j, :, cols])
            g_wide = spread_heads(qg[j, :, more])
            gkv_ref[rows, cols] = jnp.dot(slope, q_wide, preferred_element_type=F32).astype(BF16)
            gkv_ref[rows, more] = jnp.dot(low, g_wide, preferred_element_type=F32).astype(BF16)
        return 0

    lax.fori_loop(0, n, second, 0, unroll=4)

    def partial(u, i):
        weights = wfull[u * 4 + i].reshape(256, 1024)
        return lax.dot_general(gkv_ref[...], weights, NT, preferred_element_type=F32)

    def reduce_copy(stage, side, k):
        return remote(sbuf.at[stage, side, k], rbuf.at[stage, side, k],
                      rs.at[stage, side, k], rr.at[stage, side, k], mp=sides[side])

    def part_copy(i):
        j = lax.rem(e + i, n)
        return remote(parts.at[j], arrived.at[e], ps.at[i], pr.at[i], enc=j)

    def part_of(i, _):
        j = lax.rem(e + i, n)
        mine = rowq[...] == j
        for g in range(2):
            cols = pl.ds(g * WIDE, WIDE)
            more = pl.ds(512 + g * WIDE, WIDE)
            for left_ref, other, put in ((p_ref, more, cols), (slope_ref, cols, more)):
                square = lax.dot_general(
                    jnp.where(mine, left_ref[:, cols], jnp.zeros((), BF16)), kv_ref[:, other], TN,
                    preferred_element_type=F32,
                )
                part = square[0:HEAD_DIM] * head_mask(0, F32)
                for h in range(1, GROUP):
                    part = part + square[h * HEAD_DIM:(h + 1) * HEAD_DIM] * head_mask(h, F32)
                parts[j, :, put] = part.astype(BF16)

        @pl.when(i < n)
        def _():
            part_copy(i).start()

        return 0

    plan = (((far, 0), (far, 2)), ((right, 2), (left, 0)), ((right, 0), (left, 2)))
    for stage in range(3):
        if stage == 2:
            lax.fori_loop(1, n + 1, part_of, 0)

        def send(k, _, stage=stage):
            for side in range(2):
                u, base = plan[stage][side]
                term = partial(u, base + k).astype(BF16)
                if stage == 2:
                    reduce_copy(0, side, k).wait_recv()
                    term = (term.astype(F32) + rbuf[0, side, k].astype(F32)).astype(BF16)
                sbuf[stage, side, k] = term
                reduce_copy(stage, side, k).start()
            return 0

        lax.fori_loop(0, 2, send, 0)

    def mine(i, _):
        own[i] = partial(m, i).astype(BF16)
        return 0

    lax.fori_loop(0, 4, mine, 0)

    def gather_copy(u, i, side):
        return remote(obuf.at[u, i], obuf.at[u, i], gs.at[side, i], gr.at[side, i], mp=sides[side])

    def pass_on(u, k, side):
        i = 2 * side + k
        return remote(obuf.at[u, i], obuf.at[u, i], fs.at[side, k], fr.at[side, k], mp=sides[side])

    def write_out(u, i):
        return pltpu.make_async_copy(obuf.at[u, i], out_hbm.at[u, i], out_sem.at[u, i])

    def total(k, _):
        for half in range(2):
            i = 2 * half + k
            reduce_copy(2, half, k).wait_recv()
            reduce_copy(1, 1 - half, k).wait_recv()
            value = own[i].astype(F32) + rbuf[2, half, k].astype(F32)
            value = value + rbuf[1, 1 - half, k].astype(F32)
            obuf[m, i] = value.astype(BF16)
            gather_copy(m, i, half).start()
            gather_copy(m, i, 1 - half).start()
            write_out(m, i).start()
        return 0

    lax.fori_loop(0, 2, total, 0)

    def forward(k, _):
        gather_copy(left, k, 0).wait_recv()
        pass_on(left, k, 0).start()
        write_out(left, k).start()
        gather_copy(right, 2 + k, 1).wait_recv()
        pass_on(right, k, 1).start()
        write_out(right, 2 + k).start()
        return 0

    lax.fori_loop(0, 2, forward, 0)

    def collect(i, _):
        part_copy(i).wait_recv()
        return 0

    own_part = pltpu.make_async_copy(parts.at[e], arrived.at[e], part_sem)
    own_part.start()
    own_part.wait()
    lax.fori_loop(1, n, collect, 0)
    for half, put in enumerate((ctx_ref, gq_ref)):
        cols = pl.ds(half * 512, 512)
        put[...] = lax.fori_loop(
            1, n, lambda i, so_far: so_far + arrived[i, :, cols].astype(F32),
            arrived[0, :, cols].astype(F32),
        ).astype(BF16)

    def rest(k, _):
        gather_copy(left, 2 + k, 0).wait_recv()
        write_out(left, 2 + k).start()
        gather_copy(right, k, 1).wait_recv()
        write_out(right, k).start()
        return 0

    lax.fori_loop(0, 2, rest, 0)

    def last(k, _):
        pass_on(far, k, 0).wait_recv()
        write_out(far, k).start()
        pass_on(far, k, 1).wait_recv()
        write_out(far, 2 + k).start()
        return 0

    lax.fori_loop(0, 2, last, 0)

    def finish(k, _):
        for side in range(2):
            for stage in range(3):
                reduce_copy(stage, side, k).wait_send()
            gather_copy(m, k, side).wait_send()
            gather_copy(m, 2 + k, side).wait_send()
            pass_on(left if side == 0 else right, k, side).wait_send()
        for u in range(4):
            write_out(u, k).wait()
            write_out(u, 2 + k).wait()
        return 0

    lax.fori_loop(0, 2, finish, 0)

    def finish_parts(i, _):
        part_copy(i).wait_send()
        return 0

    lax.fori_loop(1, n, finish_parts, 0)

    def finish_gather(k, _):
        for copy in x_copies(k):
            copy.wait_send()
        s_copy(k).wait_send()
        sq_copy(k).wait_send()

        @pl.when(k > 0)
        def _():
            z_copy(e, k, z_up).wait_send()
            v_copy(e, k, z_up).wait_send()
            q_copy(e, k, z_up).wait_send()

        return 0

    lax.fori_loop(0, nz, finish_gather, 0)
    for copy in w_copies():
        copy.wait_send()
    for i in range(1, n):
        to_owner(i).wait_send()
        from_owner(i).wait_send()


def whole(owner, encoded, key_weight, value_weight, queries, grad_context):
    hbm = pl.BlockSpec(memory_space=pltpu.HBM)
    vmem = pl.BlockSpec(memory_space=pltpu.VMEM)
    dma = pltpu.SemaphoreType.DMA
    return pl.pallas_call(
        whole_kernel,
        out_shape=(
            jax.ShapeDtypeStruct((4, 4, 512, 256), BF16),
            jax.ShapeDtypeStruct((64, 512), BF16),
            jax.ShapeDtypeStruct((64, 512), BF16),
        ),
        in_specs=[pl.BlockSpec(memory_space=pltpu.SMEM)] + [hbm] * 5,
        out_specs=(hbm, vmem, vmem),
        scratch_shapes=[
            pltpu.VMEM((4, 4, 512, 256), BF16),
            pltpu.VMEM((512, 4096), BF16),
            pltpu.VMEM((16, 4, 64, 1024), BF16),
            pltpu.VMEM((16, 64, 1024), BF16),
            pltpu.VMEM((512, 1024), F32),
            pltpu.VMEM((512, 1024), BF16),
            pltpu.VMEM((512, 1024), BF16),
            pltpu.VMEM((512, 512), BF16),
            pltpu.VMEM((512, 512), BF16),
        ]
        + [pltpu.VMEM((512, 512), F32)] * 2
        + [pltpu.VMEM((16, 512), F32)] * 6
        + [pltpu.VMEM((16, 4, 512), F32)] * 3
        + [
            pltpu.VMEM((512, 1), jnp.int32),
            pltpu.VMEM((3, 2, 2, 512, 256), BF16),
            pltpu.VMEM((3, 2, 2, 512, 256), BF16),
            pltpu.VMEM((4, 512, 256), BF16),
            pltpu.VMEM((16, 64, 1024), BF16),
            pltpu.VMEM((16, 64, 1024), BF16),
            dma((4,)), dma,
            dma((8,)), dma((8,)), dma((8,)), dma((8,)), dma((8,)), dma((8,)),
            dma((8, 4)), dma((8, 4)), dma((4,)), dma((4,)),
            dma((8,)), dma((8,)), dma((8,)), dma((8,)),
            dma((16,)), dma((16,)), dma((16,)), dma((16,)), dma,
            dma((3, 2, 2)), dma((3, 2, 2)),
            dma((2, 4)), dma((2, 4)),
            dma((2, 2)), dma((2, 2)),
            dma((16,)), dma((16,)), dma, dma((4, 4)),
        ],
        compiler_params=pltpu.CompilerParams(
            collective_id=1, has_side_effects=True, vmem_limit_bytes=60 * MIB
        ),
        cost_estimate=pl.CostEstimate(
            flops=4 * 512 * 4096 * 1024, bytes_accessed=30 * MIB, transcendentals=0
        ),
    )(owner, encoded, key_weight, value_weight, queries, grad_context)


def place_kernel(pieces, ctx, gq, out_hbm, ctx_hbm, gq_hbm, held, heads, in_sem, out_sem):
    reads, writes = [], []
    for i in range(16):
        u, piece = i // 4, i % 4
        reads.append(pltpu.make_async_copy(pieces.at[u, piece], held.at[i], in_sem.at[i]))
        writes.append(
            pltpu.make_async_copy(
                held.at[i], out_hbm.at[:, pl.ds(i * 256, 256)], out_sem.at[i]
            )
        )
    for i, (source, target) in enumerate(((ctx, ctx_hbm), (gq, gq_hbm))):
        reads.append(pltpu.make_async_copy(source, heads.at[i], in_sem.at[16 + i]))
        writes.append(pltpu.make_async_copy(heads.at[i], target, out_sem.at[16 + i]))
    for copy in reads:
        copy.start()
    for read, write in zip(reads, writes):
        read.wait()
        write.start()
    for copy in writes:
        copy.wait()


def place(pieces, ctx, gq):
    hbm = pl.BlockSpec(memory_space=pltpu.HBM)
    small = jax.ShapeDtypeStruct((64, 512), BF16)
    return pl.pallas_call(
        place_kernel,
        out_shape=(jax.ShapeDtypeStruct((512, 4096), BF16), small, small),
        in_specs=[hbm] * 3,
        out_specs=(hbm, hbm, hbm),
        scratch_shapes=[
            pltpu.VMEM((16, 512, 256), BF16),
            pltpu.VMEM((2, 64, 512), BF16),
            pltpu.SemaphoreType.DMA((18,)),
            pltpu.SemaphoreType.DMA((18,)),
        ],
        compiler_params=pltpu.CompilerParams(vmem_limit_bytes=63 * MIB),
    )(pieces, ctx, gq)


def on_device(encoded, owner, key_weight, value_weight, queries, grad_context):
    slots, length, width = encoded.shape
    pieces, context, grad_queries = whole(
        owner, encoded.reshape(slots * length, width), key_weight, value_weight, queries,
        grad_context,
    )
    grad_encoded, context, grad_queries = place(pieces, context, grad_queries)
    return context[None], grad_queries[None], grad_encoded.reshape(encoded.shape)


def solution(mesh):
    rows = P(("enc", "dec"), None, None)
    cut = P(("enc", "dec"), None, "mp")
    weight = P(("enc", "dec"), "mp")
    return jax.shard_map(
        on_device,
        mesh=mesh,
        in_specs=(rows, P(("enc", "dec")), weight, weight, cut, cut),
        out_specs=(cut, cut, rows),
        check_vma=False,
    )
```

time: 160 us -> 148 us (0.925)
  Pallas kernels: 154 us -> 147 us
  local copies, waits for them, and re-layouts: 4.4 us -> 0 us
    pallas_call x4 -> x2, Pallas kernels: 154 us -> 147 us  [the longest x1 143 us: whole(): pl.pallas_call(whole_kernel, out_shape=(jax.ShapeDtypeStruct((4, 4, 512,...]
    unnamed x8 -> x0, local copies, waits for them, and re-layouts: 4.07 us -> none
where the time goes in v3:
time: 148 us
  Pallas kernels  147 us (99%)
    pallas_call x1, Pallas kernels, whole(): pl.pallas_call(whole_kernel, out_shape=(jax.ShapeDtypeStruct((4, 4, 512,...  143 us
    pallas_call x1, Pallas kernels, place(): pl.pallas_call(place_kernel, out_shape=(jax.ShapeDtypeStruct((512, 4096),...  3.92 us

profile of v3, /device:TPU:1, one launch (start us, length us, event | category | flops | bytes accessed | tf_op | source)
XLA Modules:
  0.0 147.8 jit_solution(1277648816228525535)
XLA Ops:
  0.6 143.3 %shard_map.85 = (bf16[4,4,512,256]{3,2,1,0:T(8,128)(2,1)}, bf16[64,512]{1,0:T(8,128)(2,1)}, bf16[64,512]{1,0:T(8,128)(2,1)}) custom-call(s32[16]{0:T(128)} %owner.1, bf16[512,4096]{1,0:T(8,128)(2,1)} %bitcast.4, bf16[64,512]{1,0:T(8,128)(2,1)} %kw_hbm.1, bf16[64,512]{1,0:T(8,128)(2,1)} %vw_hbm.1, bf16[1,64,512]{2,1,0:T(8,128)(2,1)} %q_hbm.1, ...), custom_call_target="tpu_custom_call" | custom-call | flops 8589934592 | bytes 31457280 | tf_op jit(solution)/shard_map/pallas_call | solution.py:529
  143.9 3.9 %shard_map.86 = (bf16[512,4096]{1,0:T(8,128)(2,1)}, bf16[64,512]{1,0:T(8,128)(2,1)}, bf16[64,512]{1,0:T(8,128)(2,1)}) custom-call(bf16[4,4,512,256]{3,2,1,0:T(8,128)(2,1)} %get-tuple-element.9.pieces, bf16[64,512]{1,0:T(8,128)(2,1)} %get-tuple-element.10.ctx, bf16[64,512]{1,0:T(8,128)(2,1)} %get-tuple-element.11.gq), custom_call_target="tpu_custom_call" | custom-call | tf_op jit(solution)/shard_map/pallas_call | solution.py:603

commit v4 on v3

--- a/solution.py
+++ b/solution.py
@@ -14,6 +14,14 @@
 MIB = 1024 * 1024
 BF16 = jnp.bfloat16
 F32 = jnp.float32
+
+ORDER = (
+    "W0", "A0", "B0", "X0", "A1", "W1", "X1", "W2", "X2", "F0", "A2", "W3", "T0", "Q1", "X3",
+    "W4", "X4", "V2", "F2", "W5", "N0", "W6", "V1", "X6", "S0", "Q2", "F1", "F3", "Q3", "V4",
+    "T2", "W7", "T1", "X7", "X5", "F4", "M0", "Q4", "S2", "V3", "S1", "V6", "F6", "T3", "T4",
+    "F7", "Q5", "N3", "S3", "Q6", "F5", "T5", "T6", "M2", "N4", "S4", "S6", "V5", "M3", "V7",
+    "S7", "M1", "S5", "N5", "M4", "Q7", "T7", "N6", "M7", "N2", "M6", "M5", "N7", "N1",
+)
 
 NT = (((1,), (1,)), ((), ()))
 TN = (((0,), (0,)), ((), ()))
@@ -51,7 +59,7 @@
     owner, enc_hbm, kw_hbm, vw_hbm, q_hbm, g_hbm,
     out_hbm, ctx_ref, gq_ref,
     obuf, enc, wfull, qg, acc, kv_ref, gkv_ref, p_ref, slope_ref,
-    s_scr, gc_scr, m_scr, l_scr, d_scr, mq_scr, lq_scr, dq_scr, out_st, in_st, fin_st, rowq,
+    s_scr, gc_scr, m_scr, l_scr, d_scr, mq_scr, dq_scr, out_st, in_st, fin_st, rowq,
     sbuf, rbuf, own, parts, arrived,
     load_sem, enc_sem,
     zs, zr, vs, vr, qs, qr, xs, xr, ws, wr, ss, sr, sqs, sqr,
@@ -92,8 +100,7 @@
 
     def block_of(k):
         half = (k + 1) // 2
-        offset = jnp.where(k % 2 == 1, -half, half)
-        return lax.rem(z + offset + nz, nz) * 2 + c
+        return lax.rem(z + nz + (-half if k % 2 == 1 else half), nz) * 2 + c
 
     def z_copy(b, slot, where):
         part = wfull.at[b, x, :, first_cols]
@@ -135,119 +142,77 @@
         rows = enc[:, pl.ds(pl.multiple_of(b * 256, 256), 256)]
         acc[...] += jnp.dot(rows, wfull[b].reshape(256, 1024), preferred_element_type=F32)
 
-    w_copies()[0].start()
-    w_copies()[1].start()
-    z_copy(e, 1, z_up).start()
-    z_copy(e, 2, z_down).start()
     acc[...] = jnp.zeros_like(acc)
-
-    def every(low, k, high):
-        return jnp.logical_and(k >= low, k <= high)
-
-    def step(k, _):
-        odd = k % 2 == 1
-
-        @pl.when(k < nz)
-        def _():
-            b = block_of(k)
-
-            @pl.when(k > 0)
-            def _():
+    for name in ORDER:
+        kind, k = name[0], int(name[1])
+        b = block_of(k)
+        up, down = k % 2 == 1, k % 2 == 0 and k > 0
+        if kind == "W":
+            if k == 0:
+                z_copy(e, 1, z_up).start()
+                z_copy(e, 2, z_down).start()
+            else:
                 z_copy(b, k, z_up).wait_recv()
-
-            @pl.when(jnp.logical_and(odd, k < 7))
-            def _():
+            if up and k < 7:
                 z_copy(b, k + 2, z_up).start()
-
-            @pl.when(jnp.logical_and(jnp.logical_not(odd), every(2, k, 4)))
-            def _():
+            if down and k < 5:
                 z_copy(b, k + 2, z_down).start()
-
-            one, two, _, _ = x_copies(k)
-            one.start()
-            two.start()
-
-        @pl.when(k == 1)
-        def _():
-            one, two, three, four = w_copies()
+        if kind == "X":
+            for copy in x_copies(k)[:2]:
+                copy.start()
+        if kind == "F":
+            one, two, three, four = x_copies(k)
             one.wait_recv()
             three.start()
             two.wait_recv()
             four.start()
-
-        @pl.when(k == 2)
-        def _():
-            _, _, three, four = w_copies()
+        if kind == "A":
+            one, two, three, four = w_copies()
+            if k == 0:
+                one.start()
+                two.start()
+            if k == 1:
+                one.wait_recv()
+                three.start()
+                two.wait_recv()
+                four.start()
+            if k == 2:
+                three.wait_recv()
+                four.wait_recv()
+                v_copy(e, 1, z_up).start()
+                v_copy(e, 2, z_down).start()
+        if kind == "V":
+            v_copy(b, k, z_up).wait_recv()
+            if up and k < 5:
+                v_copy(b, k + 2, z_up).start()
+            if down and k < 5:
+                v_copy(b, k + 2, z_down).start()
+            if k == 6:
+                v_copy(b, 7, z_down).start()
+        if kind == "B":
+            q_copy(e, 1, z_up).start()
+            q_copy(e, 2, z_down).start()
+        if kind == "Q":
+            q_copy(b, k, z_up).wait_recv()
+            if up and k < 7:
+                q_copy(b, k + 2, z_up).start()
+            if down and k < 5:
+                q_copy(b, k + 2, z_down).start()
+        if kind == "S":
+            if k == 0:
+                enc_load.wait()
+            _, _, three, four = x_copies(k)
             three.wait_recv()
             four.wait_recv()
-            v_copy(e, 1, z_up).start()
-            v_copy(e, 2, z_down).start()
-            q_copy(e, 1, z_up).start()
-            q_copy(e, 2, z_down).start()
-
-        @pl.when(every(2, k, nz + 1))
-        def _():
-            one, two, three, four = x_copies(k - 2)
-            one.wait_recv()
-            three.start()
-            two.wait_recv()
-            four.start()
-
-        @pl.when(every(3, k, nz + 2))
-        def _():
-            at = k - 3
-            b = block_of(at)
-
-            @pl.when(at > 0)
-            def _():
-                v_copy(b, at, z_up).wait_recv()
-
-            @pl.when(jnp.logical_and(at % 2 == 1, at < 5))
-            def _():
-                v_copy(b, at + 2, z_up).start()
-
-            @pl.when(jnp.logical_and(at % 2 == 0, every(2, at, 4)))
-            def _():
-                v_copy(b, at + 2, z_down).start()
-
-            @pl.when(at == 6)
-            def _():
-                v_copy(b, 7, z_down).start()
-
-            _, _, three, four = x_copies(at)
-            three.wait_recv()
-            four.wait_recv()
-            s_copy(at).start()
-
-            @pl.when(at == 0)
-            def _():
-                enc_load.wait()
-
+            s_copy(k).start()
             multiply(b)
-
-            @pl.when(at > 0)
-            def _():
-                q_copy(b, at, z_up).wait_recv()
-
-            @pl.when(jnp.logical_and(at % 2 == 1, at < 7))
-            def _():
-                q_copy(b, at + 2, z_up).start()
-
-            @pl.when(jnp.logical_and(at % 2 == 0, every(2, at, 4)))
-            def _():
-                q_copy(b, at + 2, z_down).start()
-
-            sq_copy(at).start()
-
-        @pl.when(k > 3)
-        def _():
-            s_copy(k - 4).wait_recv()
-            multiply(block_of(k - 4) + 1 - 2 * c)
-            sq_copy(k - 4).wait_recv()
-
-        return 0
-
-    lax.fori_loop(0, nz + 4, step, 0)
+        if kind == "M":
+            s_copy(k).wait_recv()
+            multiply(b + 1 - 2 * c)
+        if kind == "T":
+            sq_copy(k).start()
+        if kind == "N":
+            sq_copy(k).wait_recv()
     kv_ref[...] = acc[...].astype(BF16)
 
     def question(p):
@@ -289,13 +254,13 @@
         mine = lane_q == question(p)
         total = total + jnp.where(mine, scale * l_scr[pl.ds(p, 1), :], 0.0)
         delta = delta + jnp.where(mine, scale * d_scr[pl.ds(p, 1), :], 0.0)
-    lq_scr[...] = total
-    dq_scr[...] = delta
+    held = total > 0.0
+    safe = jnp.where(held, total, 1.0)
+    mq_scr[...] = jnp.where(held, peak + jnp.log(safe), LOW)
+    dq_scr[...] = delta / safe
     for j in range(n):
         out_st[j, pl.ds(0, 1), :] = mq_scr[pl.ds(j, 1), :]
-        out_st[j, pl.ds(1, 1), :] = lq_scr[pl.ds(j, 1), :]
-        out_st[j, pl.ds(2, 1), :] = dq_scr[pl.ds(j, 1), :]
-        out_st[j, pl.ds(3, 1), :] = dq_scr[pl.ds(j, 1), :]
+        out_st[j, pl.ds(1, 1), :] = dq_scr[pl.ds(j, 1), :]
 
     def to_owner(i):
         return remote(out_st.at[peer(i)], in_st.at[e], as_.at[i], ar.at[i], enc=peer(i))
@@ -305,7 +270,8 @@
 
     own_st = pltpu.make_async_copy(out_st.at[e], in_st.at[e], own_sem)
     own_st.start()
-    for i in range(1, n):
+    outward = sorted(range(1, n), key=lambda i: abs(i - 8))
+    for i in outward:
         to_owner(i).start()
     own_st.wait()
     for i in range(1, n):
@@ -318,14 +284,11 @@
     delta = jnp.zeros((1, 512), F32)
     for i in range(n):
         scale = jnp.exp(in_st[i, pl.ds(0, 1), :] - peak)
-        total = total + scale * in_st[i, pl.ds(1, 1), :]
-        delta = delta + scale * in_st[i, pl.ds(2, 1), :]
-    inverse = 1.0 / total
-    fin_st[e, pl.ds(0, 1), :] = peak
-    fin_st[e, pl.ds(1, 1), :] = inverse
-    fin_st[e, pl.ds(2, 1), :] = delta * inverse
-    fin_st[e, pl.ds(3, 1), :] = inverse
-    for i in range(1, n):
+        total = total + scale
+        delta = delta + scale * in_st[i, pl.ds(1, 1), :]
+    fin_st[e, pl.ds(0, 1), :] = peak + jnp.log(total)
+    fin_st[e, pl.ds(1, 1), :] = delta / total
+    for i in outward:
         from_owner(i).start()
     for i in range(1, n):
         from_owner(i).wait_recv()
@@ -337,10 +300,9 @@
         for g in range(2):
             cols = pl.ds(g * WIDE, WIDE)
             more = pl.ds(512 + g * WIDE, WIDE)
-            peak = fin_st[j, pl.ds(0, 1), cols]
-            inverse = fin_st[j, pl.ds(1, 1), cols] * live
-            delta = fin_st[j, pl.ds(2, 1), cols]
-            chances = jnp.exp(jnp.minimum(s_scr[rows, cols] - peak, 0.0)) * inverse
+            level = fin_st[j, pl.ds(0, 1), cols]
+            delta = fin_st[j, pl.ds(1, 1), cols]
+            chances = jnp.exp(jnp.minimum(s_scr[rows, cols] - level, 0.0)) * live
             low = chances.astype(BF16)
             slope = (chances * (gc_scr[rows, cols] - delta)).astype(BF16)
             p_ref[rows, cols] = low
@@ -351,11 +313,11 @@
             gkv_ref[rows, more] = jnp.dot(low, g_wide, preferred_element_type=F32).astype(BF16)
         return 0
 
-    lax.fori_loop(0, n, second, 0, unroll=4)
-
-    def partial(u, i):
-        weights = wfull[u * 4 + i].reshape(256, 1024)
-        return lax.dot_general(gkv_ref[...], weights, NT, preferred_element_type=F32)
+
+    def partial(u, h, k):
+        rows = pl.ds(pl.multiple_of(k * 256, 256), 256)
+        weights = wfull[pl.ds(u * 4 + 2 * h, 2)].reshape(512, 1024)
+        return lax.dot_general(gkv_ref[rows, :], weights, NT, preferred_element_type=F32)
 
     def reduce_copy(stage, side, k):
         return remote(sbuf.at[stage, side, k], rbuf.at[stage, side, k],
@@ -387,26 +349,35 @@
 
         return 0
 
-    plan = (((far, 0), (far, 2)), ((right, 2), (left, 0)), ((right, 0), (left, 2)))
-    for stage in range(3):
-        if stage == 2:
-            lax.fori_loop(1, n + 1, part_of, 0)
-
-        def send(k, _, stage=stage):
-            for side in range(2):
-                u, base = plan[stage][side]
-                term = partial(u, base + k).astype(BF16)
-                if stage == 2:
-                    reduce_copy(0, side, k).wait_recv()
-                    term = (term.astype(F32) + rbuf[0, side, k].astype(F32)).astype(BF16)
-                sbuf[stage, side, k] = term
-                reduce_copy(stage, side, k).start()
-            return 0
-
-        lax.fori_loop(0, 2, send, 0)
+    plan = (((far, 0), (far, 1)), ((right, 1), (left, 0)), ((right, 0), (left, 1)))
+
+    def send(stage, k):
+        for side in range(2):
+            u, h = plan[stage][side]
+            term = partial(u, h, k).astype(BF16)
+            if stage == 2:
+                reduce_copy(0, side, k).wait_recv()
+                term = (term.astype(F32) + rbuf[0, side, k].astype(F32)).astype(BF16)
+            sbuf[stage, side, k] = term
+            reduce_copy(stage, side, k).start()
+
+    def early(k, _):
+        lax.fori_loop(0, 8, lambda i, state: second(8 * k + i, state), 0, unroll=4)
+        send(0, k)
+        send(1, k)
+        return 0
+
+    lax.fori_loop(0, 2, early, 0)
+    lax.fori_loop(1, n + 1, part_of, 0)
+
+    def late(k, _):
+        send(2, k)
+        return 0
+
+    lax.fori_loop(0, 2, late, 0)
 
     def mine(i, _):
-        own[i] = partial(m, i).astype(BF16)
+        own[i] = partial(m, i // 2, i % 2).astype(BF16)
         return 0
 
     lax.fori_loop(0, 4, mine, 0)
@@ -500,21 +471,15 @@
 
     lax.fori_loop(1, n, finish_parts, 0)
 
-    def finish_gather(k, _):
+    for k in range(nz):
         for copy in x_copies(k):
             copy.wait_send()
         s_copy(k).wait_send()
         sq_copy(k).wait_send()
-
-        @pl.when(k > 0)
-        def _():
+        if k > 0:
             z_copy(e, k, z_up).wait_send()
             v_copy(e, k, z_up).wait_send()
             q_copy(e, k, z_up).wait_send()
-
-        return 0
-
-    lax.fori_loop(0, nz, finish_gather, 0)
     for copy in w_copies():
         copy.wait_send()
     for i in range(1, n):
@@ -529,14 +494,14 @@
     return pl.pallas_call(
         whole_kernel,
         out_shape=(
-            jax.ShapeDtypeStruct((4, 4, 512, 256), BF16),
+            jax.ShapeDtypeStruct((4, 4, 256, 512), BF16),
             jax.ShapeDtypeStruct((64, 512), BF16),
             jax.ShapeDtypeStruct((64, 512), BF16),
         ),
         in_specs=[pl.BlockSpec(memory_space=pltpu.SMEM)] + [hbm] * 5,
         out_specs=(hbm, vmem, vmem),
         scratch_shapes=[
-            pltpu.VMEM((4, 4, 512, 256), BF16),
+            pltpu.VMEM((4, 4, 256, 512), BF16),
             pltpu.VMEM((512, 4096), BF16),
             pltpu.VMEM((16, 4, 64, 1024), BF16),
             pltpu.VMEM((16, 64, 1024), BF16),
@@ -547,13 +512,13 @@
             pltpu.VMEM((512, 512), BF16),
         ]
         + [pltpu.VMEM((512, 512), F32)] * 2
-        + [pltpu.VMEM((16, 512), F32)] * 6
-        + [pltpu.VMEM((16, 4, 512), F32)] * 3
+        + [pltpu.VMEM((16, 512), F32)] * 5
+        + [pltpu.VMEM((16, 2, 512), F32)] * 3
         + [
             pltpu.VMEM((512, 1), jnp.int32),
-            pltpu.VMEM((3, 2, 2, 512, 256), BF16),
-            pltpu.VMEM((3, 2, 2, 512, 256), BF16),
-            pltpu.VMEM((4, 512, 256), BF16),
+            pltpu.VMEM((3, 2, 2, 256, 512), BF16),
+            pltpu.VMEM((3, 2, 2, 256, 512), BF16),
+            pltpu.VMEM((4, 256, 512), BF16),
             pltpu.VMEM((16, 64, 1024), BF16),
             pltpu.VMEM((16, 64, 1024), BF16),
             dma((4,)), dma,
@@ -580,11 +545,9 @@
     for i in range(16):
         u, piece = i // 4, i % 4
         reads.append(pltpu.make_async_copy(pieces.at[u, piece], held.at[i], in_sem.at[i]))
-        writes.append(
-            pltpu.make_async_copy(
-                held.at[i], out_hbm.at[:, pl.ds(i * 256, 256)], out_sem.at[i]
-            )
-        )
+        rows = pl.ds(piece % 2 * 256, 256)
+        cols = pl.ds(u * 1024 + piece // 2 * 512, 512)
+        writes.append(pltpu.make_async_copy(held.at[i], out_hbm.at[rows, cols], out_sem.at[i]))
     for i, (source, target) in enumerate(((ctx, ctx_hbm), (gq, gq_hbm))):
         reads.append(pltpu.make_async_copy(source, heads.at[i], in_sem.at[16 + i]))
         writes.append(pltpu.make_async_copy(heads.at[i], target, out_sem.at[16 + i]))
@@ -606,7 +569,7 @@
         in_specs=[hbm] * 3,
         out_specs=(hbm, hbm, hbm),
         scratch_shapes=[
-            pltpu.VMEM((16, 512, 256), BF16),
+            pltpu.VMEM((16, 256, 512), BF16),
             pltpu.VMEM((2, 64, 512), BF16),
             pltpu.SemaphoreType.DMA((18,)),
             pltpu.SemaphoreType.DMA((18,)),

time: 148 us -> 137 us (0.926)
  Pallas kernels: 147 us -> 136 us
    pallas_call x1, Pallas kernels: 143 us -> 132 us  [whole(): pl.pallas_call(whole_kernel, out_shape=(jax.ShapeDtypeStruct((4, 4, 256,...]
where the time goes in v4:
time: 137 us
  Pallas kernels  136 us (99%)
    pallas_call x1, Pallas kernels, whole(): pl.pallas_call(whole_kernel, out_shape=(jax.ShapeDtypeStruct((4, 4, 256,...  132 us
    pallas_call x1, Pallas kernels, place(): pl.pallas_call(place_kernel, out_shape=(jax.ShapeDtypeStruct((512, 4096),...  3.92 us

profile of v4, /device:TPU:1, one launch (start us, length us, event | category | flops | bytes accessed | tf_op | source)
XLA Modules:
  0.0 136.8 jit_solution(13896611872238341523)
XLA Ops:
  0.6 132.2 %shard_map.85 = (bf16[4,4,256,512]{3,2,1,0:T(8,128)(2,1)}, bf16[64,512]{1,0:T(8,128)(2,1)}, bf16[64,512]{1,0:T(8,128)(2,1)}) custom-call(s32[16]{0:T(128)} %owner.1, bf16[512,4096]{1,0:T(8,128)(2,1)} %bitcast.4, bf16[64,512]{1,0:T(8,128)(2,1)} %kw_hbm.1, bf16[64,512]{1,0:T(8,128)(2,1)} %vw_hbm.1, bf16[1,64,512]{2,1,0:T(8,128)(2,1)} %q_hbm.1, ...), custom_call_target="tpu_custom_call" | custom-call | flops 8589934592 | bytes 31457280 | tf_op jit(solution)/shard_map/pallas_call | solution.py:494
  132.8 3.9 %shard_map.86 = (bf16[512,4096]{1,0:T(8,128)(2,1)}, bf16[64,512]{1,0:T(8,128)(2,1)}, bf16[64,512]{1,0:T(8,128)(2,1)}) custom-call(bf16[4,4,256,512]{3,2,1,0:T(8,128)(2,1)} %get-tuple-element.9.pieces, bf16[64,512]{1,0:T(8,128)(2,1)} %get-tuple-element.10.ctx, bf16[64,512]{1,0:T(8,128)(2,1)} %get-tuple-element.11.gq), custom_call_target="tpu_custom_call" | custom-call | tf_op jit(solution)/shard_map/pallas_call | solution.py:566

commit v5 on v4

--- a/solution.py
+++ b/solution.py
@@ -93,7 +93,7 @@
     enc_load.start()
     greet(
         [{"dec": x_up}, {"dec": x_down}, {"mp": right}, {"mp": left}]
-        + [{"enc": peer(i)} for i in range(1, n)]
+        + [{"enc": z_up}, {"enc": z_down}, {"enc": other}]
     )
     for load in loads:
         load.wait()
@@ -239,7 +239,7 @@
             d_scr[pl.ds(p, 1), cols] = jnp.sum(raised * grads, axis=0, keepdims=True)
         return 0
 
-    lax.fori_loop(0, n, first, 0, unroll=4)
+    lax.fori_loop(0, n, first, 0, unroll=16)
 
     lane_q = lax.broadcasted_iota(jnp.int32, (n, 512), 0)
     peak = jnp.full((n, 512), LOW, F32)
@@ -362,7 +362,7 @@
             reduce_copy(stage, side, k).start()
 
     def early(k, _):
-        lax.fori_loop(0, 8, lambda i, state: second(8 * k + i, state), 0, unroll=4)
+        lax.fori_loop(0, 8, lambda i, state: second(8 * k + i, state), 0, unroll=8)
         send(0, k)
         send(1, k)
         return 0

time: 137 us -> 135 us (0.985)
  Pallas kernels: 136 us -> 134 us
    pallas_call x1, Pallas kernels: 132 us -> 130 us  [whole(): pl.pallas_call(whole_kernel, out_shape=(jax.ShapeDtypeStruct((4, 4, 256,...]
where the time goes in v5:
time: 135 us
  Pallas kernels  134 us (99%)
    pallas_call x1, Pallas kernels, whole(): pl.pallas_call(whole_kernel, out_shape=(jax.ShapeDtypeStruct((4, 4, 256,...  130 us
    pallas_call x1, Pallas kernels, place(): pl.pallas_call(place_kernel, out_shape=(jax.ShapeDtypeStruct((512, 4096),...  3.92 us

profile of v5, /device:TPU:1, one launch (start us, length us, event | category | flops | bytes accessed | tf_op | source)
XLA Modules:
  0.0 134.5 jit_solution(11813658536908155650)
XLA Ops:
  0.6 130.0 %shard_map.85 = (bf16[4,4,256,512]{3,2,1,0:T(8,128)(2,1)}, bf16[64,512]{1,0:T(8,128)(2,1)}, bf16[64,512]{1,0:T(8,128)(2,1)}) custom-call(s32[16]{0:T(128)} %owner.1, bf16[512,4096]{1,0:T(8,128)(2,1)} %bitcast.4, bf16[64,512]{1,0:T(8,128)(2,1)} %kw_hbm.1, bf16[64,512]{1,0:T(8,128)(2,1)} %vw_hbm.1, bf16[1,64,512]{2,1,0:T(8,128)(2,1)} %q_hbm.1, ...), custom_call_target="tpu_custom_call" | custom-call | flops 8589934592 | bytes 31457280 | tf_op jit(solution)/shard_map/pallas_call | solution.py:494
  130.6 3.9 %shard_map.86 = (bf16[512,4096]{1,0:T(8,128)(2,1)}, bf16[64,512]{1,0:T(8,128)(2,1)}, bf16[64,512]{1,0:T(8,128)(2,1)}) custom-call(bf16[4,4,256,512]{3,2,1,0:T(8,128)(2,1)} %get-tuple-element.9.pieces, bf16[64,512]{1,0:T(8,128)(2,1)} %get-tuple-element.10.ctx, bf16[64,512]{1,0:T(8,128)(2,1)} %get-tuple-element.11.gq), custom_call_target="tpu_custom_call" | custom-call | tf_op jit(solution)/shard_map/pallas_call | solution.py:566

commit v6 on v5

v6 whole, which is shorter than its diff:
```python
import functools

import jax
import jax.numpy as jnp
from jax import lax
from jax.experimental import pallas as pl
from jax.experimental.pallas import tpu as pltpu
from jax.sharding import PartitionSpec as P

HEAD_DIM = 64
GROUP = 4
WIDE = GROUP * HEAD_DIM
LOW = -1e30
MIB = 1024 * 1024
BF16 = jnp.bfloat16
F32 = jnp.float32

ORDER = (
    "W0", "A0", "X0", "B0", "A1", "W2", "W1", "X2", "F0", "A2", "X1", "Y0", "T0", "F2", "W3",
    "X3", "N0", "Q1", "W4", "F1", "V2", "Q2", "X4", "V1", "W6", "X6", "V4", "T2", "W5", "F4",
    "X5", "Q3", "S0", "V3", "S2", "T3", "F6", "S1", "Q4", "S4", "W7", "M2", "X7", "T4", "N3",
    "F5", "V6", "Q5", "F3", "F7", "S6", "N4", "T5", "T1", "V5", "E0", "S5", "Q6", "I0", "T6",
    "M4", "V7", "S3", "Q7", "S7", "M5", "T7", "N6", "N2", "M1", "N1", "M0", "M6", "M3", "M7",
    "N7", "N5", "K0", "U0", "K1", "Z1", "I1", "Z2", "I2", "K2", "P0", "P1", "C0", "Z3", "Z4",
    "C1", "U1", "Z5", "Z6", "I4", "G0", "R0", "R1", "y0", "y1", "Z7", "U4", "U2", "H1", "I3",
    "H0", "a1", "R4", "l0", "H4", "o0", "l1", "a0", "O0", "R2", "o1", "O1", "U3", "H2", "l2",
    "R3", "D0", "L1", "H3", "J0", "J1", "l3", "L0", "L2", "L3",
)

FOR_ALL = (0, 1, 2, 7)
NT = (((1,), (1,)), ((), ()))
TN = (((0,), (0,)), ((), ()))


def remote(src, dst, send_sem, recv_sem, **where):
    return pltpu.make_async_remote_copy(
        src_ref=src,
        dst_ref=dst,
        send_sem=send_sem,
        recv_sem=recv_sem,
        device_id=where,
        device_id_type=pl.DeviceIdType.MESH,
    )


def greet(partners):
    barrier = pltpu.get_barrier_semaphore()
    for where in partners:
        pl.semaphore_signal(barrier, inc=1, device_id=where, device_id_type=pl.DeviceIdType.MESH)
    pl.semaphore_wait(barrier, len(partners))


def head_mask(h, dtype):
    lane = lax.broadcasted_iota(jnp.int32, (1, WIDE), 1)
    inside = jnp.logical_and(lane >= h * HEAD_DIM, lane < (h + 1) * HEAD_DIM)
    return jnp.where(inside, 1.0, 0.0).astype(dtype)


def spread_heads(block):
    return jnp.concatenate([block * head_mask(h, BF16) for h in range(GROUP)], axis=0)


def whole_kernel(
    owner, enc_hbm, kw_hbm, vw_hbm, q_hbm, g_hbm,
    out_hbm, ctx_ref, gq_ref,
    obuf, enc, wfull, qg, acc, kv_ref, gkv_ref, p_ref, slope_ref,
    s_scr, gc_scr, m_scr, l_scr, d_scr, mq_scr, dq_scr, out_st, in_st, fin_st, rowq,
    pairs, wx, passing, near, parts, halves, arrived,
    load_sem, enc_sem,
    zs, zr, vs, vr, qs, qr, xs, xr, ws, wr, ss, sr, sqs, sqr,
    as_, ar, bs, br, own_sem,
    eys, eyr, ezs, ezr, exs, exr, ess, esr, keep_sem,
    hs, hr, ks, kr, gs, gr, fs, fr, cs, cr, ps, pr, part_sem, out_sem,
):
    e = lax.axis_index("enc")
    x = lax.axis_index("dec")
    m = lax.axis_index("mp")
    n, nz, nx, ny = 16, 8, 4, 4
    z, c = e // 2, e % 2
    other = e + 1 - 2 * c
    z_up, z_down = lax.rem(z + 1, nz) * 2 + c, lax.rem(z + nz - 1, nz) * 2 + c
    x_up, x_down = lax.rem(x + 1, nx), lax.rem(x + nx - 1, nx)
    right, left, far = lax.rem(m + 1, ny), lax.rem(m + 3, ny), lax.rem(m + 2, ny)
    sides = (right, left)

    def peer(i):
        return lax.rem(e + i, n)

    first_cols, last_cols = pl.ds(0, 768), pl.ds(768, 256)
    enc_load = pltpu.make_async_copy(enc_hbm, enc, enc_sem)
    loads = [
        pltpu.make_async_copy(kw_hbm, wfull.at[e, x, :, pl.ds(0, 512)], load_sem.at[0]),
        pltpu.make_async_copy(vw_hbm, wfull.at[e, x, :, pl.ds(512, 512)], load_sem.at[1]),
        pltpu.make_async_copy(q_hbm.at[0], qg.at[e, :, pl.ds(0, 512)], load_sem.at[2]),
        pltpu.make_async_copy(g_hbm.at[0], qg.at[e, :, pl.ds(512, 512)], load_sem.at[3]),
    ]
    for load in loads:
        load.start()
    enc_load.start()
    greet(
        [{"dec": x_up}, {"dec": x_down}, {"mp": right}, {"mp": left}]
        + [{"enc": z_up}, {"enc": z_down}, {"enc": other}, {"mp": far}]
    )
    for load in loads:
        load.wait()

    def block_of(k):
        half = (k + 1) // 2
        return lax.rem(z + nz + (-half if k % 2 == 1 else half), nz) * 2 + c

    def z_copy(b, slot, where):
        part = wfull.at[b, x, :, first_cols]
        return remote(part, part, zs.at[slot], zr.at[slot], enc=where)

    def v_copy(b, slot, where):
        part = wfull.at[b, :, :, last_cols]
        return remote(part, part, vs.at[slot], vr.at[slot], enc=where)

    def q_copy(b, slot, where):
        return remote(qg.at[b], qg.at[b], qs.at[slot], qr.at[slot], enc=where)

    def x_four(b, cols, send, recv):
        whole = wfull.at[b, x, :, cols]
        low = wfull.at[b, x_down, pl.ds(0, 32), cols]
        high = wfull.at[b, x_up, pl.ds(32, 32), cols]
        return (
            remote(whole, whole, send(0), recv(0), dec=x_up),
            remote(whole, whole, send(1), recv(1), dec=x_down),
            remote(low, low, send(2), recv(2), dec=x_up),
            remote(high, high, send(3), recv(3), dec=x_down),
        )

    def x_copies(k):
        return x_four(block_of(k), first_cols, lambda i: xs.at[k, i], lambda i: xr.at[k, i])

    def w_copies():
        return x_four(e, last_cols, lambda i: ws.at[i], lambda i: wr.at[i])

    def s_copy(k):
        b = block_of(k)
        return remote(wfull.at[b], wfull.at[b], ss.at[k], sr.at[k], enc=other)

    def sq_copy(k):
        b = block_of(k)
        return remote(qg.at[b], qg.at[b], sqs.at[k], sqr.at[k], enc=other)

    def multiply(b):
        rows = enc[:, pl.ds(pl.multiple_of(b * 256, 256), 256)]
        acc[...] += jnp.dot(rows, wfull[b].reshape(256, 1024), preferred_element_type=F32)

    def slot_z(k):
        half = (k + 1) // 2
        return lax.rem(z + nz + jnp.where(k % 2 == 1, -half, half), nz)

    def shard_of(s, k):
        if 3 <= k <= 6:
            return passing.at[s, k - 3]
        return wx.at[s, FOR_ALL.index(k), c, x]

    def ey_copies():
        shard = wfull.at[e, x]
        return (
            remote(shard, wx.at[1, 0, c, x], eys.at[0], eyr.at[1], mp=right),
            remote(shard, wx.at[0, 0, c, x], eys.at[1], eyr.at[0], mp=left),
            remote(shard, wx.at[2, 0, c, x], eys.at[2], eyr.at[2], mp=far),
        )

    def ez_copy(s, slot):
        return remote(
            shard_of(s, max(slot - 2, 0)), shard_of(s, slot),
            ezs.at[s, slot], ezr.at[s, slot], enc=z_up if slot % 2 == 1 else z_down,
        )

    def ez_step(slot):
        for s in range(3):
            ez_copy(s, slot).wait_recv()
            if slot < 6:
                ez_copy(s, slot + 2).start()

    def ex_copies(s, p):
        whole = wx.at[s, p, c, x]
        mine = passing.at[s, m] if p == 4 else whole
        low = wx.at[s, p, c, x_down, pl.ds(0, 32)]
        high = wx.at[s, p, c, x_up, pl.ds(32, 32)]
        return (
            remote(mine, whole, exs.at[s, p, 0], exr.at[s, p, 0], dec=x_up),
            remote(mine, whole, exs.at[s, p, 1], exr.at[s, p, 1], dec=x_down),
            remote(low, low, exs.at[s, p, 2], exr.at[s, p, 2], dec=x_up),
            remote(high, high, exs.at[s, p, 3], exr.at[s, p, 3], dec=x_down),
        )

    def es_copy(s, p):
        return remote(wx.at[s, p, c], wx.at[s, p, c], ess.at[s, p], esr.at[s, p], enc=other)

    def keep_copy(s):
        return pltpu.make_async_copy(passing.at[s, m], wx.at[s, 4, c, x], keep_sem.at[s])

    def ex_send(p):
        for s in range(3):
            if p == 4:
                keep_copy(s).start()
            for copy in ex_copies(s, p)[:2]:
                copy.start()

    def ex_pass(p):
        for s in range(3):
            one, two, three, four = ex_copies(s, p)
            one.wait_recv()
            three.start()
            two.wait_recv()
            four.start()

    def es_send(p):
        for s in range(3):
            if p == 4:
                keep_copy(s).wait()
            for copy in ex_copies(s, p)[2:]:
                copy.wait_recv()
            es_copy(s, p).start()

    def es_wait(p):
        for s in range(3):
            es_copy(s, p).wait_recv()

    def to_owner(i):
        return remote(out_st.at[peer(i)], in_st.at[e], as_.at[i], ar.at[i], enc=peer(i))

    def from_owner(i):
        return remote(fin_st.at[e], fin_st.at[e], bs.at[i], br.at[i], enc=peer(i))

    def question(p):
        held = owner[p]
        return jnp.where(held >= 0, held // nx, -1)

    def first(p, _):
        j = jnp.maximum(question(p), 0)
        rows = pl.ds(pl.multiple_of(p * 32, 32), 32)
        rowq[rows, :] = jnp.full((32, 1), question(p), jnp.int32)
        for g in range(2):
            cols = pl.ds(g * WIDE, WIDE)
            more = pl.ds(512 + g * WIDE, WIDE)
            q_wide = spread_heads(qg[j, :, cols])
            g_wide = spread_heads(qg[j, :, more])
            scores = lax.dot_general(kv_ref[rows, cols], q_wide, NT, preferred_element_type=F32)
            grads = lax.dot_general(kv_ref[rows, more], g_wide, NT, preferred_element_type=F32)
            s_scr[rows, cols] = scores
            gc_scr[rows, cols] = grads
            peak = jnp.max(scores, axis=0, keepdims=True)
            raised = jnp.exp(scores - peak)
            m_scr[pl.ds(p, 1), cols] = peak
            l_scr[pl.ds(p, 1), cols] = jnp.sum(raised, axis=0, keepdims=True)
            d_scr[pl.ds(p, 1), cols] = jnp.sum(raised * grads, axis=0, keepdims=True)
        return 0

    def second(p, _):
        j = jnp.maximum(question(p), 0)
        live = jnp.where(question(p) >= 0, 1.0, 0.0)
        rows = pl.ds(pl.multiple_of(p * 32, 32), 32)
        for g in range(2):
            cols = pl.ds(g * WIDE, WIDE)
            more = pl.ds(512 + g * WIDE, WIDE)
            level = fin_st[j, pl.ds(0, 1), cols]
            delta = fin_st[j, pl.ds(1, 1), cols]
            chances = jnp.exp(jnp.minimum(s_scr[rows, cols] - level, 0.0)) * live
            low = chances.astype(BF16)
            slope = (chances * (gc_scr[rows, cols] - delta)).astype(BF16)
            p_ref[rows, cols] = low
            slope_ref[rows, cols] = slope
            q_wide = spread_heads(qg[j, :, cols])
            g_wide = spread_heads(qg[j, :, more])
            gkv_ref[rows, cols] = jnp.dot(slope, q_wide, preferred_element_type=F32).astype(BF16)
            gkv_ref[rows, more] = jnp.dot(low, g_wide, preferred_element_type=F32).astype(BF16)
        return 0


    def pair_copy(k, side):
        rows = pl.ds(k * 256, 256)
        return remote(gkv_ref.at[rows], pairs.at[1 - side, rows], hs.at[side, k], hr.at[side, k],
                      mp=sides[side])

    def pair_pass(side):
        rows = pl.ds(side * 256, 256)
        return remote(pairs.at[1 - side, rows], pairs.at[2, rows], ks.at[side], kr.at[side],
                      mp=sides[side])

    def product(slot, place, rows, s):
        weights = wfull[pl.ds(2 * slot_z(slot), 2)] if s == 3 else wx[s, place]
        left_side = gkv_ref[rows, :] if s == 3 else pairs[s, rows, :]
        term = lax.dot_general(
            left_side, weights.reshape(512, 1024), NT, preferred_element_type=F32
        )
        return term.astype(BF16).astype(F32)

    def near_terms(slot, place, k):
        rows = pl.ds(pl.multiple_of(k * 256, 256), 256)
        total = product(slot, place, rows, 3)
        for s in range(2):
            total = total + product(slot, place, rows, s)
        near[place, k] = total

    def far_term(slot, place, k):
        rows = pl.ds(pl.multiple_of(k * 256, 256), 256)
        obuf[slot, k] = (near[place, k] + product(slot, place, rows, 2)).astype(BF16)

    def core_copy(h):
        j = lax.rem(e + 2 * h + 1, n)
        return remote(parts.at[j], halves.at[j // 2], cs.at[h], cr.at[h], enc=other)

    def part_copy(h):
        j = lax.rem(e + 2 * h + 2, n)
        return remote(parts.at[j], arrived.at[z], ps.at[h], pr.at[h], enc=j)

    def part_of(j):
        mine = rowq[...] == j
        for g in range(2):
            cols = pl.ds(g * WIDE, WIDE)
            more = pl.ds(512 + g * WIDE, WIDE)
            for left_ref, other, put in ((p_ref, more, cols), (slope_ref, cols, more)):
                square = lax.dot_general(
                    jnp.where(mine, left_ref[:, cols], jnp.zeros((), BF16)), kv_ref[:, other], TN,
                    preferred_element_type=F32,
                )
                part = square[0:HEAD_DIM] * head_mask(0, F32)
                for h in range(1, GROUP):
                    part = part + square[h * HEAD_DIM:(h + 1) * HEAD_DIM] * head_mask(h, F32)
                parts[j, :, put] = part.astype(BF16)

    def part_pair(h, _):
        part_of(lax.rem(e + 2 * h + 1, n))
        core_copy(h).start()
        part_of(lax.rem(e + 2 * h + 2, n))
        return 0

    def part_merge(h, _):
        j = lax.rem(e + 2 * h + 2, n)
        both = parts[j].astype(F32) + halves[j // 2].astype(F32)
        parts[j] = both.astype(BF16)

        @pl.when(h < 7)
        def _():
            part_copy(h).start()

        return 0

    def core_wait(h, _):
        core_copy(h).wait_recv()
        return 0

    mine = 3 + m

    def gather_copy(u, k, side):
        return remote(obuf.at[u, k], obuf.at[u, k], gs.at[side, k], gr.at[side, k], mp=sides[side])

    def pass_on(u, side):
        return remote(obuf.at[u, side], obuf.at[u, side], fs.at[side], fr.at[side], mp=sides[side])

    def write_out(u, k):
        return pltpu.make_async_copy(obuf.at[u, k], out_hbm.at[slot_z(u), k], out_sem.at[u, k])

    outward = sorted(range(1, n), key=lambda i: abs(i - 8))
    own_st = pltpu.make_async_copy(out_st.at[e], in_st.at[e], own_sem)
    acc[...] = jnp.zeros_like(acc)
    loaded = False
    for name in ORDER:
        kind, k = name[0], int(name[1])
        b = block_of(k)
        up, down = k % 2 == 1, k % 2 == 0 and k > 0
        if kind == "W":
            if k == 0:
                z_copy(e, 1, z_up).start()
                z_copy(e, 2, z_down).start()
            else:
                z_copy(b, k, z_up).wait_recv()
            if up and k < 7:
                z_copy(b, k + 2, z_up).start()
            if down and k < 5:
                z_copy(b, k + 2, z_down).start()
        if kind == "X":
            for copy in x_copies(k)[:2]:
                copy.start()
        if kind == "F":
            one, two, three, four = x_copies(k)
            one.wait_recv()
            three.start()
            two.wait_recv()
            four.start()
        if kind == "A":
            one, two, three, four = w_copies()
            if k == 0:
                one.start()
                two.start()
            if k == 1:
                one.wait_recv()
                three.start()
                two.wait_recv()
                four.start()
            if k == 2:
                three.wait_recv()
                four.wait_recv()
                v_copy(e, 1, z_up).start()
                v_copy(e, 2, z_down).start()
        if kind == "V":
            v_copy(b, k, z_up).wait_recv()
            if up and k < 5:
                v_copy(b, k + 2, z_up).start()
            if down and k < 5:
                v_copy(b, k + 2, z_down).start()
            if k == 6:
                v_copy(b, 7, z_down).start()
        if kind == "B":
            q_copy(e, 1, z_up).start()
            q_copy(e, 2, z_down).start()
        if kind == "Q":
            q_copy(b, k, z_up).wait_recv()
            if up and k < 7:
                q_copy(b, k + 2, z_up).start()
            if down and k < 5:
                q_copy(b, k + 2, z_down).start()
        if kind == "S":
            if not loaded:
                enc_load.wait()
                loaded = True
            _, _, three, four = x_copies(k)
            three.wait_recv()
            four.wait_recv()
            s_copy(k).start()
            multiply(b)
        if kind == "M":
            s_copy(k).wait_recv()
            multiply(b + 1 - 2 * c)
        if kind == "T":
            sq_copy(k).start()
        if kind == "N":
            sq_copy(k).wait_recv()
        if kind == "Y":
            for copy in ey_copies():
                copy.start()
        if kind == "E":
            for s in (1, 0, 2):
                remote(wfull.at[e, x], wx.at[s, 0, c, x], eys.at[s], eyr.at[s], mp=right).wait_recv()
                ez_copy(s, 1).start()
                ez_copy(s, 2).start()
        if kind == "I":
            ex_send(k)
        if kind == "U":
            ex_pass(k)
        if kind == "R":
            es_send(k)
        if kind == "H":
            es_wait(k)
        if kind == "Z":
            ez_step(k)
        if name == "K0":
            kv_ref[...] = acc[...].astype(BF16)
            lax.fori_loop(0, n, first, 0, unroll=16)

            lane_q = lax.broadcasted_iota(jnp.int32, (n, 512), 0)
            peak = jnp.full((n, 512), LOW, F32)
            for p in range(n):
                peak = jnp.maximum(peak, jnp.where(lane_q == question(p), m_scr[pl.ds(p, 1), :], LOW))
            mq_scr[...] = peak
            total = jnp.zeros((n, 512), F32)
            delta = jnp.zeros((n, 512), F32)
            for p in range(n):
                j = jnp.maximum(question(p), 0)
                scale = jnp.exp(jnp.minimum(m_scr[pl.ds(p, 1), :] - mq_scr[pl.ds(j, 1), :], 0.0))
                here = lane_q == question(p)
                total = total + jnp.where(here, scale * l_scr[pl.ds(p, 1), :], 0.0)
                delta = delta + jnp.where(here, scale * d_scr[pl.ds(p, 1), :], 0.0)
            held = total > 0.0
            safe = jnp.where(held, total, 1.0)
            mq_scr[...] = jnp.where(held, peak + jnp.log(safe), LOW)
            dq_scr[...] = delta / safe
            for j in range(n):
                out_st[j, pl.ds(0, 1), :] = mq_scr[pl.ds(j, 1), :]
                out_st[j, pl.ds(1, 1), :] = dq_scr[pl.ds(j, 1), :]

            own_st.start()
            for i in outward:
                to_owner(i).start()
        if name == "K1":
            own_st.wait()
            for i in range(1, n):
                to_owner(i).wait_recv()
            peak = in_st[0, pl.ds(0, 1), :]
            for i in range(1, n):
                peak = jnp.maximum(peak, in_st[i, pl.ds(0, 1), :])
            total = jnp.zeros((1, 512), F32)
            delta = jnp.zeros((1, 512), F32)
            for i in range(n):
                scale = jnp.exp(in_st[i, pl.ds(0, 1), :] - peak)
                total = total + scale
                delta = delta + scale * in_st[i, pl.ds(1, 1), :]
            fin_st[e, pl.ds(0, 1), :] = peak + jnp.log(total)
            fin_st[e, pl.ds(1, 1), :] = delta / total
            for i in outward:
                from_owner(i).start()
        if name == "K2":
            for i in range(1, n):
                from_owner(i).wait_recv()
        if kind == "P":
            lax.fori_loop(0, 8, lambda i, state, k=k: second(8 * k + i, state), 0, unroll=8)
            pair_copy(k, 0).start()
            pair_copy(k, 1).start()
        if kind == "C":
            lax.fori_loop(4 * k, 4 * k + 4, part_pair, 0)
        if kind == "G":
            lax.fori_loop(0, 8, core_wait, 0)
            lax.fori_loop(0, 8, part_merge, 0)
        if kind == "y":
            pair_copy(k, k).wait_recv()
            pair_pass(k).start()
        if kind == "a":
            for side in range(2):
                if k == 1:
                    pair_copy(1 - side, side).wait_recv()
                if k == 0:
                    pair_pass(side).wait_recv()
        if kind == "l":
            for half in range(2):
                near_terms(FOR_ALL[k], k, half)
        if kind == "L":
            for half in range(2):
                far_term(FOR_ALL[k], k, half)
                write_out(FOR_ALL[k], half).start()
        if kind == "o":
            near_terms(mine, 4, k)
        if kind == "O":
            far_term(mine, 4, k)
            gather_copy(mine, k, 0).start()
            gather_copy(mine, k, 1).start()
            write_out(mine, k).start()
        if kind == "J":
            u = 3 + sides[1 - k]
            gather_copy(u, k, k).wait_recv()
            pass_on(u, k).start()
            write_out(u, k).start()
        if kind == "D":
            def collect(i, _):
                part_copy(i).wait_recv()
                return 0

            own_part = pltpu.make_async_copy(parts.at[e], arrived.at[z], part_sem)
            own_part.start()
            own_part.wait()
            lax.fori_loop(0, 7, collect, 0)
            for half, put in enumerate((ctx_ref, gq_ref)):
                cols = pl.ds(half * 512, 512)
                put[...] = lax.fori_loop(
                    1, nz, lambda i, so_far: so_far + arrived[i, :, cols].astype(F32),
                    arrived[0, :, cols].astype(F32),
                ).astype(BF16)


    gather_copy(3 + left, 1, 0).wait_recv()
    write_out(3 + left, 1).start()
    gather_copy(3 + right, 0, 1).wait_recv()
    write_out(3 + right, 0).start()
    for side in range(2):
        pass_on(3 + far, side).wait_recv()
        write_out(3 + far, side).start()

    for side in range(2):
        pair_pass(side).wait_send()
        pass_on(mine, side).wait_send()
        for k in range(2):
            pair_copy(k, side).wait_send()
            gather_copy(mine, k, side).wait_send()
    for u in range(8):
        for k in range(2):
            write_out(u, k).wait()
    for copy in ey_copies():
        copy.wait_send()
    for slot in range(1, 8):
        for s in range(3):
            ez_copy(s, slot).wait_send()
    for s in range(3):
        for p in range(5):
            es_copy(s, p).wait_send()
            for copy in ex_copies(s, p):
                copy.wait_send()

    for h in range(8):
        core_copy(h).wait_send()
        if h < 7:
            part_copy(h).wait_send()
    for k in range(nz):
        for copy in x_copies(k):
            copy.wait_send()
        s_copy(k).wait_send()
        sq_copy(k).wait_send()
        if k > 0:
            z_copy(e, k, z_up).wait_send()
            v_copy(e, k, z_up).wait_send()
            q_copy(e, k, z_up).wait_send()
    for copy in w_copies():
        copy.wait_send()
    for i in range(1, n):
        to_owner(i).wait_send()
        from_owner(i).wait_send()


def whole(owner, encoded, key_weight, value_weight, queries, grad_context):
    hbm = pl.BlockSpec(memory_space=pltpu.HBM)
    vmem = pl.BlockSpec(memory_space=pltpu.VMEM)
    dma = pltpu.SemaphoreType.DMA
    return pl.pallas_call(
        whole_kernel,
        out_shape=(
            jax.ShapeDtypeStruct((8, 2, 256, 512), BF16),
            jax.ShapeDtypeStruct((64, 512), BF16),
            jax.ShapeDtypeStruct((64, 512), BF16),
        ),
        in_specs=[pl.BlockSpec(memory_space=pltpu.SMEM)] + [hbm] * 5,
        out_specs=(hbm, vmem, vmem),
        scratch_shapes=[
            pltpu.VMEM((8, 2, 256, 512), BF16),
            pltpu.VMEM((512, 4096), BF16),
            pltpu.VMEM((16, 4, 64, 1024), BF16),
            pltpu.VMEM((16, 64, 1024), BF16),
            pltpu.VMEM((512, 1024), F32),
            pltpu.VMEM((512, 1024), BF16),
            pltpu.VMEM((512, 1024), BF16),
            pltpu.VMEM((512, 512), BF16),
            pltpu.VMEM((512, 512), BF16),
        ]
        + [pltpu.VMEM((512, 512), F32)] * 2
        + [pltpu.VMEM((16, 512), F32)] * 5
        + [pltpu.VMEM((16, 2, 512), F32)] * 3
        + [
            pltpu.VMEM((512, 1), jnp.int32),
            pltpu.VMEM((3, 512, 1024), BF16),
            pltpu.VMEM((3, 5, 2, 4, 64, 1024), BF16),
            pltpu.VMEM((3, 4, 64, 1024), BF16),
            pltpu.VMEM((5, 2, 256, 512), F32),
            pltpu.VMEM((16, 64, 1024), BF16),
            pltpu.VMEM((8, 64, 1024), BF16),
            pltpu.VMEM((8, 64, 1024), BF16),
            dma((4,)), dma,
            dma((8,)), dma((8,)), dma((8,)), dma((8,)), dma((8,)), dma((8,)),
            dma((8, 4)), dma((8, 4)), dma((4,)), dma((4,)),
            dma((8,)), dma((8,)), dma((8,)), dma((8,)),
            dma((16,)), dma((16,)), dma((16,)), dma((16,)), dma,
            dma((3,)), dma((3,)), dma((3, 8)), dma((3, 8)),
            dma((3, 5, 4)), dma((3, 5, 4)), dma((3, 5)), dma((3, 5)), dma((3,)),
            dma((2, 2)), dma((2, 2)), dma((2,)), dma((2,)),
            dma((2, 2)), dma((2, 2)), dma((2,)), dma((2,)),
            dma((8,)), dma((8,)), dma((8,)), dma((8,)), dma, dma((8, 2)),
        ],
        compiler_params=pltpu.CompilerParams(
            collective_id=1, has_side_effects=True, vmem_limit_bytes=60 * MIB
        ),
        cost_estimate=pl.CostEstimate(
            flops=4 * 512 * 4096 * 1024, bytes_accessed=30 * MIB, transcendentals=0
        ),
    )(owner, encoded, key_weight, value_weight, queries, grad_context)


def place_kernel(pieces, ctx, gq, out_hbm, ctx_hbm, gq_hbm, held, heads, in_sem, out_sem):
    reads, writes = [], []
    for i in range(16):
        u, k = i // 2, i % 2
        reads.append(pltpu.make_async_copy(pieces.at[u, k], held.at[i], in_sem.at[i]))
        rows = pl.ds(k * 256, 256)
        cols = pl.ds(u * 512, 512)
        writes.append(pltpu.make_async_copy(held.at[i], out_hbm.at[rows, cols], out_sem.at[i]))
    for i, (source, target) in enumerate(((ctx, ctx_hbm), (gq, gq_hbm))):
        reads.append(pltpu.make_async_copy(source, heads.at[i], in_sem.at[16 + i]))
        writes.append(pltpu.make_async_copy(heads.at[i], target, out_sem.at[16 + i]))
    for copy in reads:
        copy.start()
    for read, write in zip(reads, writes):
        read.wait()
        write.start()
    for copy in writes:
        copy.wait()


def place(pieces, ctx, gq):
    hbm = pl.BlockSpec(memory_space=pltpu.HBM)
    small = jax.ShapeDtypeStruct((64, 512), BF16)
    return pl.pallas_call(
        place_kernel,
        out_shape=(jax.ShapeDtypeStruct((512, 4096), BF16), small, small),
        in_specs=[hbm] * 3,
        out_specs=(hbm, hbm, hbm),
        scratch_shapes=[
            pltpu.VMEM((16, 256, 512), BF16),
            pltpu.VMEM((2, 64, 512), BF16),
            pltpu.SemaphoreType.DMA((18,)),
            pltpu.SemaphoreType.DMA((18,)),
        ],
        compiler_params=pltpu.CompilerParams(vmem_limit_bytes=63 * MIB),
    )(pieces, ctx, gq)


def on_device(encoded, owner, key_weight, value_weight, queries, grad_context):
    slots, length, width = encoded.shape
    pieces, context, grad_queries = whole(
        owner, encoded.reshape(slots * length, width), key_weight, value_weight, queries,
        grad_context,
    )
    grad_encoded, context, grad_queries = place(pieces, context, grad_queries)
    return context[None], grad_queries[None], grad_encoded.reshape(encoded.shape)


def solution(mesh):
    rows = P(("enc", "dec"), None, None)
    cut = P(("enc", "dec"), None, "mp")
    weight = P(("enc", "dec"), "mp")
    return jax.shard_map(
        on_device,
        mesh=mesh,
        in_specs=(rows, P(("enc", "dec")), weight, weight, cut, cut),
        out_specs=(cut, cut, rows),
        check_vma=False,
    )
```

time: 135 us -> 129 us (0.956)
  Pallas kernels: 134 us -> 128 us
    pallas_call x1, Pallas kernels: 130 us -> 124 us  [whole(): pl.pallas_call(whole_kernel, out_shape=(jax.ShapeDtypeStruct((8, 2, 256,...]
where the time goes in v6:
time: 129 us
  Pallas kernels  128 us (99%)
    pallas_call x1, Pallas kernels, whole(): pl.pallas_call(whole_kernel, out_shape=(jax.ShapeDtypeStruct((8, 2, 256,...  124 us
    pallas_call x1, Pallas kernels, place(): pl.pallas_call(place_kernel, out_shape=(jax.ShapeDtypeStruct((512, 4096),...  3.92 us

profile of v6, /device:TPU:1, one launch (start us, length us, event | category | flops | bytes accessed | tf_op | source)
XLA Modules:
  0.0 129.0 jit_solution(9590891940776170585)
XLA Ops:
  0.6 124.2 %shard_map.85 = (bf16[8,2,256,512]{3,2,1,0:T(8,128)(2,1)}, bf16[64,512]{1,0:T(8,128)(2,1)}, bf16[64,512]{1,0:T(8,128)(2,1)}) custom-call(s32[16]{0:T(128)} %owner.1, bf16[512,4096]{1,0:T(8,128)(2,1)} %bitcast.4, bf16[64,512]{1,0:T(8,128)(2,1)} %kw_hbm.1, bf16[64,512]{1,0:T(8,128)(2,1)} %vw_hbm.1, bf16[1,64,512]{2,1,0:T(8,128)(2,1)} %q_hbm.1, ...), custom_call_target="tpu_custom_call" | custom-call | flops 8589934592 | bytes 31457280 | tf_op jit(solution)/shard_map/pallas_call | solution.py:607
  124.9 3.9 %shard_map.86 = (bf16[512,4096]{1,0:T(8,128)(2,1)}, bf16[64,512]{1,0:T(8,128)(2,1)}, bf16[64,512]{1,0:T(8,128)(2,1)}) custom-call(bf16[8,2,256,512]{3,2,1,0:T(8,128)(2,1)} %get-tuple-element.9.pieces, bf16[64,512]{1,0:T(8,128)(2,1)} %get-tuple-element.10.ctx, bf16[64,512]{1,0:T(8,128)(2,1)} %get-tuple-element.11.gq), custom_call_target="tpu_custom_call" | custom-call | tf_op jit(solution)/shard_map/pallas_call | solution.py:682

commit v7 on v6

--- a/solution.py
+++ b/solution.py
@@ -16,15 +16,15 @@
 F32 = jnp.float32
 
 ORDER = (
-    "W0", "A0", "X0", "B0", "A1", "W2", "W1", "X2", "F0", "A2", "X1", "Y0", "T0", "F2", "W3",
-    "X3", "N0", "Q1", "W4", "F1", "V2", "Q2", "X4", "V1", "W6", "X6", "V4", "T2", "W5", "F4",
-    "X5", "Q3", "S0", "V3", "S2", "T3", "F6", "S1", "Q4", "S4", "W7", "M2", "X7", "T4", "N3",
-    "F5", "V6", "Q5", "F3", "F7", "S6", "N4", "T5", "T1", "V5", "E0", "S5", "Q6", "I0", "T6",
-    "M4", "V7", "S3", "Q7", "S7", "M5", "T7", "N6", "N2", "M1", "N1", "M0", "M6", "M3", "M7",
-    "N7", "N5", "K0", "U0", "K1", "Z1", "I1", "Z2", "I2", "K2", "P0", "P1", "C0", "Z3", "Z4",
-    "C1", "U1", "Z5", "Z6", "I4", "G0", "R0", "R1", "y0", "y1", "Z7", "U4", "U2", "H1", "I3",
-    "H0", "a1", "R4", "l0", "H4", "o0", "l1", "a0", "O0", "R2", "o1", "O1", "U3", "H2", "l2",
-    "R3", "D0", "L1", "H3", "J0", "J1", "l3", "L0", "L2", "L3",
+    "W0", "T0", "B0", "A0", "X0", "W2", "A1", "W1", "X1", "N0", "X2", "Y0", "A2", "W3", "W4",
+    "Q1", "X3", "F0", "V2", "X4", "W5", "F1", "Q2", "V1", "W6", "F3", "F4", "Q3", "V4", "X6",
+    "Q4", "X5", "S1", "V3", "F2", "W7", "F6", "X7", "S3", "S0", "Q5", "T2", "T4", "V6", "M1",
+    "E0", "T1", "M3", "S2", "F5", "T5", "F7", "V5", "T3", "S6", "S4", "M2", "V7", "I0", "S5",
+    "S7", "Q6", "Q7", "T7", "T6", "M0", "M4", "N2", "M5", "M6", "M7", "N5", "N4", "N6", "N7",
+    "N3", "N1", "K0", "U0", "K1", "Z1", "I1", "Z2", "R0", "K2", "P0", "P1", "I2", "Z3", "Z4",
+    "U1", "C0", "Z5", "Z6", "I4", "C1", "y0", "G0", "R1", "Z7", "y1", "U4", "a1", "I3", "R4",
+    "H0", "H4", "o0", "l0", "a0", "O0", "H1", "U3", "o1", "U2", "O1", "R3", "l1", "H3", "D0",
+    "J0", "R2", "l3", "J1", "L3", "H2", "l2", "L2", "L1", "L0",
 )
 
 FOR_ALL = (0, 1, 2, 7)

time: 129 us -> 126 us (0.977)
  Pallas kernels: 128 us -> 125 us
    pallas_call x1, Pallas kernels: 124 us -> 121 us  [whole(): pl.pallas_call(whole_kernel, out_shape=(jax.ShapeDtypeStruct((8, 2, 256,...]
where the time goes in v7:
time: 126 us
  Pallas kernels  125 us (99%)
    pallas_call x1, Pallas kernels, whole(): pl.pallas_call(whole_kernel, out_shape=(jax.ShapeDtypeStruct((8, 2, 256,...  121 us
    pallas_call x1, Pallas kernels, place(): pl.pallas_call(place_kernel, out_shape=(jax.ShapeDtypeStruct((512, 4096),...  3.92 us

profile of v7, /device:TPU:1, one launch (start us, length us, event | category | flops | bytes accessed | tf_op | source)
XLA Modules:
  0.0 125.9 jit_solution(5780247789174806833)
XLA Ops:
  0.6 121.1 %shard_map.85 = (bf16[8,2,256,512]{3,2,1,0:T(8,128)(2,1)}, bf16[64,512]{1,0:T(8,128)(2,1)}, bf16[64,512]{1,0:T(8,128)(2,1)}) custom-call(s32[16]{0:T(128)} %owner.1, bf16[512,4096]{1,0:T(8,128)(2,1)} %bitcast.4, bf16[64,512]{1,0:T(8,128)(2,1)} %kw_hbm.1, bf16[64,512]{1,0:T(8,128)(2,1)} %vw_hbm.1, bf16[1,64,512]{2,1,0:T(8,128)(2,1)} %q_hbm.1, ...), custom_call_target="tpu_custom_call" | custom-call | flops 8589934592 | bytes 31457280 | tf_op jit(solution)/shard_map/pallas_call | solution.py:607
  121.8 3.9 %shard_map.86 = (bf16[512,4096]{1,0:T(8,128)(2,1)}, bf16[64,512]{1,0:T(8,128)(2,1)}, bf16[64,512]{1,0:T(8,128)(2,1)}) custom-call(bf16[8,2,256,512]{3,2,1,0:T(8,128)(2,1)} %get-tuple-element.9.pieces, bf16[64,512]{1,0:T(8,128)(2,1)} %get-tuple-element.10.ctx, bf16[64,512]{1,0:T(8,128)(2,1)} %get-tuple-element.11.gq), custom_call_target="tpu_custom_call" | custom-call | tf_op jit(solution)/shard_map/pallas_call | solution.py:682
